TPU v7x, 512 devices: a whole 4x4x16 slice. The times are simulated.
512 devices in a mesh: seq: 64 (over z_hi, y, x, core), tp: 8 (over z_lo).
Axes of the slice: x: 4, y: 4, z: 16 (z_hi: 2, z_lo: 8; z = z_hi * 8 + z_lo), core: 2. Of those that a mesh axis runs over, the one named last changes fastest.
Arguments:
- projected: bfloat16 [3, 65536, 4096], P(None, 'seq', 'tp'), may hold values from -6 to 6
- short_taps: float32 [3, 3, 4096], P(None, None, 'tp'), may hold values from -3 to 3
- long_filter: bfloat16 [256, 128], P('tp'), may hold values from -0.5 to 0.5
- out_weight: bfloat16 [4096, 4096], P('seq', 'tp'), may hold values from -0.09375 to 0.09375
Outputs:
- mixed: bfloat16 [65536, 4096], P('seq', 'tp')
All inputs are finite; a program needn't handle non-finite values.
Results may differ from a plain program's by a relative error of at most 0.0057.
Values may be sent and summed in bfloat16 or wider, within the bound.
No kernel may reach another device: no remote copies, remote signals or barrier semaphores. Data moves between devices by JAX's collectives and lax.ppermute only.
A program may use at most 64 MiB of HBM per device.

v0:
```python
import jax
import jax.numpy as jnp
from jax import lax
from jax.sharding import PartitionSpec as P


def shifted(block, axis, distance):
    devices = range(lax.axis_size(axis))
    route = [(i - distance, i) for i in devices if i - distance in devices]
    return lax.ppermute(block, axis, route)


def toeplitz_blocks(long_filter):
    groups, taps = long_filter.shape
    rows_idx = jnp.arange(taps, dtype=jnp.int32)[:, None]
    cols_idx = jnp.arange(2 * taps, dtype=jnp.int32)[None, :]
    lag_table = rows_idx + (taps - 1) - cols_idx
    tap_index = jnp.arange(taps, dtype=jnp.int32)[:, None, None]
    selector = (lag_table[None, :, :] == tap_index).astype(jnp.bfloat16)
    blocks = jnp.einsum("gj,jab->gab", long_filter, selector, preferred_element_type=jnp.float32)
    return blocks.astype(jnp.bfloat16)


def featurize(extended, short_taps):
    tap_zero = short_taps[:, 0][:, None, :]
    tap_one = short_taps[:, 1][:, None, :]
    tap_two = short_taps[:, 2][:, None, :]
    return tap_zero * extended[:, 2:] + tap_one * extended[:, 1:-1] + tap_two * extended[:, :-2]


def grouped_conv(gated_ext, long_filter):
    groups, taps = long_filter.shape
    channels = gated_ext.shape[1]
    tokens = gated_ext.shape[0] - taps + 1
    gated_pad = jnp.concatenate([gated_ext, jnp.zeros((1, channels), jnp.bfloat16)], axis=0)
    pieces = gated_pad.reshape(tokens // taps + 1, taps, channels)
    windows = jnp.concatenate([pieces[:-1], pieces[1:]], axis=1)
    windows = windows.reshape(tokens // taps, 2 * taps, groups, channels // groups)
    conv = jnp.einsum(
        "gab,nbgc->nagc", toeplitz_blocks(long_filter), windows, preferred_element_type=jnp.float32
    )
    return conv.reshape(tokens, channels)


def per_device(projected, short_taps, long_filter, out_weight):
    taps = long_filter.shape[1]
    tokens = projected.shape[1]
    tail_rows = shifted(projected[:, tokens - 2 :], "seq", 1)
    features = featurize(jnp.concatenate([tail_rows, projected], axis=1), short_taps)
    query_feat = features[0]
    gated_in = (features[1] * features[2]).astype(jnp.bfloat16)
    gated_tail = shifted(gated_in[tokens - taps + 1 :], "seq", 1)
    gated_ext = jnp.concatenate([gated_tail, gated_in], axis=0)
    conv = grouped_conv(gated_ext, long_filter)
    gated_out = (query_feat * conv).astype(jnp.bfloat16)
    whole = lax.all_gather(gated_out, "tp", axis=1, tiled=True)
    return jnp.dot(
        whole,
        lax.all_gather(out_weight, "seq", axis=0, tiled=True),
        preferred_element_type=jnp.float32,
    ).astype(jnp.bfloat16)


def solution(mesh):
    in_specs = (P(None, "seq", "tp"), P(None, None, "tp"), P("tp", None), P("seq", "tp"))
    out_specs = P("seq", "tp")
    return jax.shard_map(
        per_device, mesh=mesh, in_specs=in_specs, out_specs=out_specs, check_vma=False
    )
```

profile of v0, /device:TPU:1, one launch (start us, length us, event | category | flops | bytes accessed | tf_op | source)
XLA Modules:
  0.0 346.0 jit_solution(16591589154682767891)
XLA Ops:
  6.5 0.7 all-gather.5.cloned.1.call-update
  7.3 0.8 slice.45
  8.1 1.0 copy.6
  9.0 4.5 %collective-permute-start = (bf16[3,2,512]{1,2,0:T(8,128)(2,1)}, bf16[3,2,512]{1,2,0:T(8,128)(2,1)S(1)}, u32[]{:S(2)}, u32[]{:S(2)}) collective-permute-start(bf16[3,2,512]{1,2,0:T(8,128)(2,1)} %copy.6), channel_id=1, source_target_pairs={{0,8},{8,16},{16,24},{24,32},{32,40},{40,48},{48,56},{56,64},{64,7... | collective-permute-start | bytes 18440 | tf_op jit(solution)/shard_map/ppermute | solution.py:10
  13.5 1.5 fusion.20
  15.1 2.5 iota_compare_fusion
  17.6 7.6 %fusion = bf16[128,256,32]{1,2,0:T(8,128)(2,1)} fusion(pred[128,128,256]{2,1,0:T(32,128)(4,1)S(1)} %iota_compare_fusion, bf16[32,128]{1,0:T(8,128)(2,1)S(1)} %copy-done), kind=kOutput, calls=%fused_computation.1 | convolution fusion | flops 268435456 | bytes 6299648 | tf_op jit(solution)/shard_map/gj,jab->gab/dot_general | solution.py:20
  25.2 0.6 copy_bitcast_fusion
  25.8 3.2 copy.5
  29.0 0.7 copy.32
  29.7 4.8 %multiply_add_fusion = f32[3,1024,512]{1,2,0:T(8,128)S(1)} fusion(bf16[3,1024,512]{1,2,0:T(8,128)(2,1)S(1)} %copy.5, bf16[3,2,512]{1,2,0:T(8,128)(2,1)S(1)} %collective-permute-done, f32[3,512]{1,0:T(4,128)S(1)} %get-tuple-element.10, f32[3,512]{1,0:T(4,128)} %get-tuple-element.11, f32[3,512]{1,0:T(4,128)S(1)} %bitcast.54), kind=kLoop, calls=%fused_computation.3 | loop fusion | flops 22020096 | bytes 9461760 | tf_op jit(solution)/shard_map/add | solution.py:28
  34.4 0.3 fusion.7
  34.9 2.1 collective-permute-start.1
  37.0 0.3 fusion.23
  37.3 3.4 collective-permute-done.1
  40.7 1.0 fusion.17
  42.2 0.3 copy.17
  42.7 0.5 copy-done.1
  43.3 1.5 fusion.11
  44.7 0.9 copy.10
  45.6 1.4 fusion.6
  47.0 109.3 %all-gather.5.cloned.1.call-done = bf16[4096,512]{1,0:T(8,128)(2,1)} async-done(((bf16[64,512]{1,0:T(8,128)(2,1)}), bf16[4096,512]{1,0:T(8,128)(2,1)}) %all-gather.5.cloned.1.call-update) | async-done | bytes 4194320 | tf_op jit(solution)/shard_map/all_gather | solution.py:59
  156.3 172.8 %all-gather.3.cloned.1.call-done = bf16[1024,4096]{0,1:T(8,128)(2,1)} async-done(((bf16[1024,512]{0,1:T(8,128)(2,1)}), bf16[1024,4096]{0,1:T(8,128)(2,1)}) %all-gather.3.cloned.1.call-update) | async-done | bytes 8388624 | tf_op jit(solution)/shard_map/all_gather | solution.py:56
  329.1 10.1 %convolution_convert_fusion = bf16[1024,512]{1,0:T(8,128)(2,1)} fusion(bf16[1024,4096]{0,1:T(8,128)(2,1)} %all-gather.3.cloned.1.call-done, bf16[4096,512]{1,0:T(8,128)(2,1)} %all-gather.5.cloned.1.call-done), kind=kOutput, calls=%fused_computation.20 | convolution fusion | flops 4295491584 | bytes 13631488 | tf_op jit(solution)/shard_map/dot_general | solution.py:57
  (13 shorter events, 1.0 us)
Async XLA Ops:
  6.5 11.1 %copy-start = (bf16[32,128]{1,0:T(8,128)(2,1)S(1)}, bf16[32,128]{1,0:T(8,128)(2,1)}, u32[]{:S(2)}) copy-start(bf16[32,128]{1,0:T(8,128)(2,1)} %param.6) | copy-start | bytes 24580
  6.5 149.7 %all-gather.5.cloned.1.call-start = ((), (), s32[]{:S(2)}) async-start(), calls=%async_computation.1 | async-start | bytes 4259840 | tf_op jit(solution)/shard_map/all_gather | solution.py:59
  7.3 321.8 %all-gather.3.cloned.1.call-start = ((), (), s32[]{:S(2)}) async-start(), calls=%async_computation | async-start | bytes 9437184 | tf_op jit(solution)/shard_map/all_gather | solution.py:56
  9.0 20.6 %collective-permute-start = (bf16[3,2,512]{1,2,0:T(8,128)(2,1)}, bf16[3,2,512]{1,2,0:T(8,128)(2,1)S(1)}, u32[]{:S(2)}, u32[]{:S(2)}) collective-permute-start(bf16[3,2,512]{1,2,0:T(8,128)(2,1)} %copy.6), channel_id=1, source_target_pairs={{0,8},{8,16},{16,24},{24,32},{32,40},{40,48},{48,56},{56,64},{64,7... | collective-permute-start | bytes 18440 | tf_op jit(solution)/shard_map/ppermute | solution.py:10
  34.9 5.8 %collective-permute-start.1 = (bf16[127,512]{0,1:T(8,128)(2,1)S(1)}, bf16[127,512]{0,1:T(8,128)(2,1)S(1)}, u32[]{:S(2)}, u32[]{:S(2)}) collective-permute-start(bf16[127,512]{0,1:T(8,128)(2,1)S(1)} %slice_bitcast_fusion.1), channel_id=1, source_target_pairs={{0,8},{8,16},{16,24},{24,32},{32,40},{40,48},{48,56},{56,64},{64,7... | collective-permute-start | bytes 390152 | tf_op jit(solution)/shard_map/ppermute | solution.py:10
  41.7 1.6 copy-start.1
Sparse Core Ops, SparseCore 0:
  11.8 144.4 all-gather.4
  158.4 170.6 all-gather.2
where the time goes:
time: 346 us
  waiting for transfers between devices  286 us (83%)
  matrix products  19.1 us (6%)
  between operations  13.5 us (4%)
  other arithmetic  10.3 us (3%)
  local copies, waits for them, and re-layouts  10.2 us (3%)
  starting transfers between devices  6.64 us (2%)
    all_gather x1, waiting for transfers between devices, per_device(): whole = lax.all_gather(gated_out, 'tp', axis=1, tiled=True)  173 us
    all_gather x1, waiting for transfers between devices, per_device(): lax.all_gather(out_weight, 'seq', axis=0, tiled=True)  109 us
    dot_general x1, matrix products, per_device(): jnp.dot(whole, lax.all_gather(out_weight, 'seq', axis=0, tiled=True), pre...  10.1 us
    dot_general x1, matrix products, toeplitz_blocks(): jnp.einsum('gj,jab->gab', long_filter, selector, preferred_element_type=j...  7.59 us
  transfers between devices with their start and end apart: 4, of which 3 were waited for; matrix products, arithmetic and copies ran while one was open for 8% of the time, Pallas kernels for 0%

commit v1 on v0

v1 whole, which is shorter than its diff:
```python
import functools

import jax
import jax.numpy as jnp
from jax import lax
from jax.experimental import pallas as pl
from jax.experimental.pallas import tpu as pltpu
from jax.sharding import Mesh, PartitionSpec as P

SEQ = ("zh", "y", "x", "c")
PLANE = ("y", "x", "c")
LINE = ("c", "tp")
HALO = 144
LANES = 128
LINE_LEN = 8
WORKERS = 4


def on_line(pairs):
    place = lambda u, core: core * LINE_LEN + (u if core == 0 else LINE_LEN - 1 - u)
    return [(place(a, core), place(b, core)) for core in (0, 1) for a, b in pairs]


def inward(block, step):
    return lax.ppermute(block, LINE, on_line([(u, u - 1) for u in range(1, LINE_LEN + 1 - step)]))


def outward(block, step):
    return lax.ppermute(block, LINE, on_line([(u, u + 1) for u in range(step - 1, WORKERS - 1)]))


def deliver(block, workers):
    return lax.ppermute(block, LINE, on_line([(u, u + WORKERS) for u in workers]))


def feature(rows, taps):
    return (
        taps[0:1] * rows
        + taps[1:2] * pltpu.roll(rows, 1, 0)
        + taps[2:3] * pltpu.roll(rows, 2, 0)
    )


def local_kernel(early, x_ref, halo_ref, taps_ref, filt_ref, out_ref, toep):
    groups, taps = filt_ref.shape[1], filt_ref.shape[2]
    half = out_ref.shape[0]
    width = LANES // groups
    lag = lax.broadcasted_iota(jnp.int32, (taps, 2 * taps), 0)
    col = lax.broadcasted_iota(jnp.int32, (taps, 2 * taps), 1)
    flip = jnp.where(lag + col == taps, 1.0, 0.0).astype(jnp.bfloat16)
    first = jnp.dot(filt_ref[0], flip, preferred_element_type=jnp.float32)
    for g in range(groups):
        wide = jnp.broadcast_to(first[g : g + 1], (taps, 2 * taps))
        wide = pltpu.roll(wide, 0, 1, stride=1, stride_axis=0)
        toep[g * taps : (g + 1) * taps] = wide.astype(jnp.bfloat16)

    def rows(stream):
        if early:
            own = x_ref[stream, :half].astype(jnp.float32)
            return jnp.concatenate([halo_ref[stream].astype(jnp.float32), own], axis=0)
        return x_ref[stream, half - HALO :].astype(jnp.float32)

    query = feature(rows(0), taps_ref[0])[HALO:]
    gated = feature(rows(1), taps_ref[1]) * feature(rows(2), taps_ref[2])
    gated = gated[HALO - taps :].astype(jnp.bfloat16)
    group_of = lax.broadcasted_iota(jnp.int32, (taps, 2 * LANES), 1) % LANES // width
    for pair in range(half // taps // 2):
        base = 2 * pair * taps
        window = jnp.concatenate(
            [gated[base : base + 2 * taps], gated[base + taps : base + 3 * taps]], axis=1
        )
        every = jnp.dot(toep[...], window, preferred_element_type=jnp.float32)
        conv = every[:taps]
        for g in range(1, groups):
            conv = jnp.where(group_of == g, every[g * taps : (g + 1) * taps], conv)
        for k in range(2):
            at = base + k * taps
            piece = conv[:, k * LANES : (k + 1) * LANES] * query[at : at + taps]
            out_ref[at : at + taps] = piece.astype(jnp.bfloat16)


def local_part(early, x, halo, short_taps, long_filter):
    streams, tokens, channels = x.shape
    groups, taps = long_filter.shape
    tiles = channels // LANES
    filt = long_filter.reshape(tiles, groups // tiles, taps)
    half = tokens // 2
    return pl.pallas_call(
        functools.partial(local_kernel, early),
        grid=(tiles,),
        in_specs=[
            pl.BlockSpec((streams, tokens, LANES), lambda i: (0, 0, i)),
            pl.BlockSpec((streams, HALO, LANES), lambda i: (0, 0, i)),
            pl.BlockSpec((streams, 3, LANES), lambda i: (0, 0, i)),
            pl.BlockSpec((1, groups // tiles, taps), lambda i: (i, 0, 0)),
        ],
        out_specs=pl.BlockSpec((half, LANES), lambda i: (0, i)),
        out_shape=jax.ShapeDtypeStruct((half, channels), jnp.bfloat16),
        scratch_shapes=[pltpu.VMEM((groups // tiles * taps, 2 * taps), jnp.bfloat16)],
        compiler_params=pltpu.CompilerParams(vmem_limit_bytes=32 << 20),
        cost_estimate=pl.CostEstimate(flops=1 << 30, bytes_accessed=4 << 20, transcendentals=0),
        name="early_tokens" if early else "late_tokens",
    )(x, halo, short_taps, filt)


def project_kernel(blocks, has_start, y_ref, z_ref, *refs):
    x_refs, w_ref = refs[: 2 * blocks], refs[2 * blocks]
    start_ref = refs[2 * blocks + 1] if has_start else None
    out_ref, acc = refs[-2:]
    step = pl.program_id(0)
    depth = x_refs[0].shape[1]
    half = x_refs[0].shape[0]
    weight = w_ref[...].reshape(depth, w_ref.shape[-1])
    for i in range(blocks):

        @pl.when(step == i)
        def _():
            for part in range(2):
                at = pl.ds(part * half, half)
                term = jnp.dot(
                    x_refs[2 * i + part][...], weight, preferred_element_type=jnp.float32
                )
                if i == 0 and has_start:
                    term = start_ref[at] + term
                elif i > 0:
                    term = acc[at] + term
                if i == blocks - 1:
                    out_ref[at] = term.astype(out_ref.dtype)
                else:
                    acc[at] = term


def project(pairs, index, weights, side, start, kind, name):
    blocks = len(pairs)
    half, depth = pairs[0][0].shape
    ys, members, zs, rows, columns = weights.shape
    columns //= 2
    whole = lambda i, y, z: (0, 0)
    in_specs = [pl.BlockSpec((half, depth), whole)] * (2 * blocks)
    in_specs.append(
        pl.BlockSpec((1, members, 1, rows, columns), lambda i, y, z: (y[i], 0, z[i], 0, side))
    )
    operands = [part for pair in pairs for part in pair] + [weights]
    if start is not None:
        in_specs.append(pl.BlockSpec((2 * half, columns), whole))
        operands.append(start)
    return pl.pallas_call(
        functools.partial(project_kernel, blocks, start is not None),
        grid_spec=pltpu.PrefetchScalarGridSpec(
            num_scalar_prefetch=2,
            grid=(blocks,),
            in_specs=in_specs,
            out_specs=pl.BlockSpec((2 * half, columns), whole),
            scratch_shapes=[pltpu.VMEM((2 * half, columns), jnp.float32)],
        ),
        out_shape=jax.ShapeDtypeStruct((2 * half, columns), kind),
        compiler_params=pltpu.CompilerParams(vmem_limit_bytes=48 << 20),
        cost_estimate=pl.CostEstimate(
            flops=4 * blocks * half * depth * columns,
            bytes_accessed=blocks * 2 * (2 * half * depth + depth * columns),
            transcendentals=0,
        ),
        name=name,
    )(index[0], index[1], *operands)


def per_device(projected, short_taps, long_filter, out_weight):
    streams, tokens, channels = projected.shape
    core, at, zh = lax.axis_index("c"), lax.axis_index("tp"), lax.axis_index("zh")
    u = jnp.where(core == 0, at, LINE_LEN - 1 - at)
    toward = jnp.where(core == 0, 1, -1)
    others = lambda hop: [(i, (i + hop) % LINE_LEN) for i in range(LINE_LEN)]
    swap_zh = [(0, 1), (1, 0)]

    far = lax.ppermute(out_weight, "zh", swap_zh)
    next_seq = [(i, i + 1) for i in range(lax.axis_size(SEQ) - 1)]
    halo = lax.ppermute(projected[:, tokens - HALO :], SEQ, next_seq)
    near_partner = lax.ppermute(out_weight, "tp", others(WORKERS))
    both = lambda z, t: z * LINE_LEN + t
    far_partner = lax.ppermute(
        out_weight,
        ("zh", "tp"),
        [(both(z, t), both(1 - z, (t + WORKERS) % LINE_LEN)) for z in (0, 1) for t in range(LINE_LEN)],
    )
    shard = jnp.concatenate(
        [
            jnp.concatenate([out_weight, near_partner], axis=1),
            jnp.concatenate([far, far_partner], axis=1),
        ],
        axis=0,
    )
    weights = lax.all_gather(shard, PLANE, axis=0, tiled=True)
    rows, columns = out_weight.shape
    weights = weights.reshape(lax.axis_size("y"), -1, 2, rows, 2 * columns)

    def rows_of(distances):
        block = jnp.stack([jnp.clip(at + toward * d, 0, LINE_LEN - 1) for d in distances])
        per_zh = lax.axis_size("y")
        return (block % per_zh).astype(jnp.int32), (block // per_zh != zh).astype(jnp.int32)

    late = local_part(False, projected, projected[:, :HALO], short_taps, long_filter)
    early = local_part(True, projected, halo, short_taps, long_filter)
    own = (early, late)

    came = [own]
    for step in range(1, LINE_LEN):
        before, behind = came[-1]
        behind = inward(behind, step)
        before = inward(before, step)
        came.append((before, behind))
    back = [own]
    for step in range(1, WORKERS):
        before, behind = back[-1]
        back.append((outward(before, step), outward(behind, step)))

    pick = lambda yes, one, other: tuple(jnp.where(yes, a, b) for a, b in zip(one, other))
    fifth = pick(u < WORKERS - 1, came[5], back[3])
    fifth_at = jnp.where(u < WORKERS - 1, 5, -3)
    first_blocks = came[:5] + [fifth, back[1], back[2]]
    first_index = rows_of([0, 1, 2, 3, 4, fifth_at, -1, -2])
    total = project(first_blocks, first_index, weights, 1, None, jnp.float32, "partner_first")
    sent_two = deliver(total.astype(jnp.bfloat16), (2, 3))
    total = project([came[6]], rows_of([6]), weights, 1, total, jnp.float32, "partner_sixth")
    sent_one = deliver(total.astype(jnp.bfloat16), (1,))
    total = project([came[7]], rows_of([7]), weights, 1, total, jnp.bfloat16, "partner_last")
    sent_last = deliver(total, (0,))

    sixth = pick(u < WORKERS - 2, came[6], back[2])
    sixth_at = jnp.where(u < WORKERS - 2, 6, -2)
    seventh = pick(u < WORKERS - 3, came[7], back[1])
    seventh_at = jnp.where(u < WORKERS - 3, 7, -1)
    own_blocks = came[:5] + [fifth, sixth, seventh]
    own_index = rows_of([0, 1, 2, 3, 4, fifth_at, sixth_at, seventh_at])
    mine = project(own_blocks, own_index, weights, 0, None, jnp.bfloat16, "own_columns")
    given = jnp.where(u == WORKERS, sent_last, jnp.where(u == WORKERS + 1, sent_one, sent_two))
    return jnp.where(u < WORKERS, mine, given)


def solution(mesh):
    split = Mesh(mesh.devices.reshape(2, 4, 4, 2, LINE_LEN), ("zh", "y", "x", "c", "tp"))
    in_specs = (P(None, SEQ, "tp"), P(None, None, "tp"), P("tp", None), P(SEQ, "tp"))
    return jax.shard_map(
        per_device, mesh=split, in_specs=in_specs, out_specs=P(SEQ, "tp"), check_vma=False
    )
```

time: 346 us -> 237 us (0.68)
  the two profiles are of different devices: /device:TPU:1 before, /device:TPU:480 now
where the time goes in v1:
time: 237 us; the launch traced here: 235 us
  waiting for transfers between devices  94.1 us (40%)
  starting transfers between devices  70 us (30%)
  Pallas kernels  34.2 us (14%)
  other arithmetic  15.4 us (6%)
  between operations  13.7 us (6%)
  local copies, waits for them, and re-layouts  7.93 us (3%)
    ppermute x3, waiting for transfers between devices, deliver(): lax.ppermute(block, LINE, on_line([(u, u + WORKERS) for u in workers]))  67.7 us
    ppermute x14, starting transfers between devices, inward(): lax.ppermute(block, LINE, on_line([(u, u - 1) for u in range(1, LINE_LEN...  39.2 us
    pallas_call x4, Pallas kernels, project(): pl.pallas_call(functools.partial(project_kernel, blocks, start is not Non...  26.2 us
    ppermute x14, waiting for transfers between devices, inward(): lax.ppermute(block, LINE, on_line([(u, u - 1) for u in range(1, LINE_LEN...  11.2 us
    select_n x6, other arithmetic, per_device(): jnp.where(yes, a, b)  10.6 us
    ppermute x6, starting transfers between devices, outward(): lax.ppermute(block, LINE, on_line([(u, u + 1) for u in range(step - 1, WO...  8.79 us
    ppermute x1, waiting for transfers between devices, per_device(): halo = lax.ppermute(projected[:, tokens - HALO:], SEQ, next_seq)  8.26 us
    ppermute x1, starting transfers between devices, per_device(): far = lax.ppermute(out_weight, 'zh', swap_zh)  8.22 us
  transfers between devices with their start and end apart: 28, of which 4 were waited for; matrix products, arithmetic and copies ran while one was open for 6% of the time, Pallas kernels for 15%

profile of v1, /device:TPU:480, one launch (start us, length us, event | category | flops | bytes accessed | tf_op | source)
XLA Modules:
  0.0 235.3 jit_solution(13607595088670450584)
XLA Ops:
  6.5 5.4 %collective-permute-start.21 = (bf16[64,512]{1,0:T(8,128)(2,1)}, bf16[64,512]{1,0:T(8,128)(2,1)S(1)}, u32[]{:S(2)}, u32[]{:S(2)}) collective-permute-start(bf16[64,512]{1,0:T(8,128)(2,1)} %param.7), channel_id=1, source_target_pairs={{0,4},{1,5},{2,6},{3,7},{4,0},{5,1},{6,2},{7,3},{8,12},{9,13},{10,... | collective-permute-start | bytes 196616 | tf_op jit(solution)/shard_map/ppermute | solution.py:178
  12.0 3.3 %collective-permute-start.23 = (bf16[64,512]{1,0:T(8,128)(2,1)}, bf16[64,512]{1,0:T(8,128)(2,1)S(1)}, u32[]{:S(2)}, u32[]{:S(2)}) collective-permute-start(bf16[64,512]{1,0:T(8,128)(2,1)} %param.7), channel_id=1, source_target_pairs={{0,260},{1,261},{2,262},{3,263},{4,256},{5,257},{6,258},{7,259},{2... | collective-permute-start | bytes 196616 | tf_op jit(solution)/shard_map/ppermute | solution.py:180
  15.3 8.2 %collective-permute-start.22 = (bf16[64,512]{1,0:T(8,128)(2,1)}, bf16[64,512]{1,0:T(8,128)(2,1)S(1)}, u32[]{:S(2)}, u32[]{:S(2)}) collective-permute-start(bf16[64,512]{1,0:T(8,128)(2,1)} %param.7), channel_id=1, source_target_pairs={{0,256},{256,0},{1,257},{257,1},{2,258},{258,2},{3,259},{259,3},{4... | collective-permute-start | bytes 196616 | tf_op jit(solution)/shard_map/ppermute | solution.py:175
  23.6 6.8 %collective-permute-done.22 = bf16[64,512]{1,0:T(8,128)(2,1)S(1)} collective-permute-done((bf16[64,512]{1,0:T(8,128)(2,1)}, bf16[64,512]{1,0:T(8,128)(2,1)S(1)}, u32[]{:S(2)}, u32[]{:S(2)}) %collective-permute-start.22) | collective-permute-done | bytes 65568 | tf_op jit(solution)/shard_map/ppermute | solution.py:175
  30.4 1.6 maximum_maximum_fusion
  33.2 1.9 collective-permute-start
  35.2 1.9 copy-done.1
  38.5 3.9 %late_tokens.1.refs_1_ = bf16[512,512]{1,0:T(8,128)(2,1)S(1)} custom-call(bf16[3,1024,512]{2,1,0:T(8,128)(2,1)S(1)} %copy-done.1, bf16[3,144,512]{2,1,0:T(8,128)(2,1)S(1)} %get-tuple-element.5.halo_ref, f32[3,3,512]{2,1,0:T(4,128)S(1)} %copy-done.8, bf16[4,8,128]{2,1,0:T(8,128)(2,1)S(1)} %bitcast.15), custom_call_target="tpu_custom_call" | custom-call | flops 1073741824 | bytes 4194304 | tf_op jit(solution)/shard_map/late_tokens/pallas_call | solution.py:88
  42.4 5.4 %collective-permute-start.2 = (bf16[512,512]{1,0:T(8,128)(2,1)S(1)}, bf16[512,512]{1,0:T(8,128)(2,1)S(1)}, u32[]{:S(2)}, u32[]{:S(2)}) collective-permute-start(bf16[512,512]{1,0:T(8,128)(2,1)S(1)} %late_tokens.1.refs_1_), channel_id=1, source_target_pairs={{1,0},{2,1},{3,2},{4,3},{5,4},{6,5},{7,6},{14,15},{13,14},{12,13},... | collective-permute-start | bytes 1572872 | tf_op jit(solution)/shard_map/ppermute | solution.py:25
  47.9 8.3 %collective-permute-done.halo_ref = bf16[3,144,512]{2,1,0:T(8,128)(2,1)S(1)} collective-permute-done((bf16[3,144,512]{2,1,0:T(8,128)(2,1)S(1)}, bf16[3,144,512]{2,1,0:T(8,128)(2,1)S(1)}, u32[]{:S(2)}, u32[]{:S(2)}) %collective-permute-start) | collective-permute-done | bytes 442400 | tf_op jit(solution)/shard_map/ppermute | solution.py:177
  56.1 4.0 %early_tokens.1.refs_0_ = bf16[512,512]{1,0:T(8,128)(2,1)S(1)} custom-call(bf16[3,1024,512]{2,1,0:T(8,128)(2,1)S(1)} %copy-done.1, bf16[3,144,512]{2,1,0:T(8,128)(2,1)S(1)} %collective-permute-done.halo_ref, f32[3,3,512]{2,1,0:T(4,128)S(1)} %copy-done.8, bf16[4,8,128]{2,1,0:T(8,128)(2,1)S(1)} %bitcast.16), custom_call_target="tpu_custom_call" | custom-call | flops 1073741824 | bytes 4194304 | tf_op jit(solution)/shard_map/early_tokens/pallas_call | solution.py:88
  60.2 18.5 %collective-permute-start.1 = (bf16[512,512]{1,0:T(8,128)(2,1)S(1)}, bf16[512,512]{1,0:T(8,128)(2,1)S(1)}, u32[]{:S(2)}, u32[]{:S(2)}) collective-permute-start(bf16[512,512]{1,0:T(8,128)(2,1)S(1)} %early_tokens.1.refs_0_), channel_id=1, source_target_pairs={{1,0},{2,1},{3,2},{4,3},{5,4},{6,5},{7,6},{14,15},{13,14},{12,13},... | collective-permute-start | bytes 1572872 | tf_op jit(solution)/shard_map/ppermute | solution.py:25
  79.4 11.2 %collective-permute-done.1.refs_2_ = bf16[512,512]{1,0:T(8,128)(2,1)S(1)} collective-permute-done((bf16[512,512]{1,0:T(8,128)(2,1)S(1)}, bf16[512,512]{1,0:T(8,128)(2,1)S(1)}, u32[]{:S(2)}, u32[]{:S(2)}) %collective-permute-start.1) | collective-permute-done | bytes 524320 | tf_op jit(solution)/shard_map/ppermute | solution.py:25
  112.2 1.9 broadcast_select_fusion.4.refs_11_
  118.2 1.9 broadcast_select_fusion.2.refs_13_
  122.1 11.2 %partner_first.1.refs_3_ = f32[1024,512]{1,0:T(8,128)} custom-call(s32[8]{0:T(128)S(1)} %and_select_fusion.1.y_ref, s32[8]{0:T(128)S(1)} %compare_convert_fusion.z_ref, bf16[512,512]{1,0:T(8,128)(2,1)S(1)} %early_tokens.1.refs_0_, bf16[512,512]{1,0:T(8,128)(2,1)S(1)} %late_tokens.1.refs_1_, bf16[512,512]{1,0:T(8,128)(2,1)S(1)} %collective-permute-done.1.refs_2_, ...), custom_call_target="tpu_custom_call" | custom-call | flops 4294967296 | bytes 12582912 | tf_op jit(solution)/shard_map/partner_first/pallas_call | solution.py:147
  133.4 1.9 convert_element_type.23
  135.6 2.1 partner_sixth.1.refs_3_
  138.6 2.1 partner_last.1
  143.1 1.9 broadcast_select_fusion.3.refs_12_
  145.0 1.9 broadcast_select_fusion.refs_15_
  146.8 1.9 broadcast_select_fusion.1.refs_14_
  148.7 10.8 %own_columns.1 = bf16[1024,512]{1,0:T(8,128)(2,1)} custom-call(s32[8]{0:T(128)S(1)} %and_select_fusion.3.y_ref, s32[8]{0:T(128)S(1)} %compare_convert_fusion.1.z_ref, bf16[512,512]{1,0:T(8,128)(2,1)S(1)} %early_tokens.1.refs_0_, bf16[512,512]{1,0:T(8,128)(2,1)S(1)} %late_tokens.1.refs_1_, bf16[512,512]{1,0:T(8,128)(2,1)S(1)} %collective-permute-done.1.refs_2_, ...), custom_call_target="tpu_custom_call" | custom-call | flops 4294967296 | bytes 12582912 | tf_op jit(solution)/shard_map/own_columns/pallas_call | solution.py:147
  159.6 67.7 %collective-permute-done.26 = bf16[1024,512]{1,0:T(8,128)(2,1)S(1)} collective-permute-done((bf16[1024,512]{1,0:T(8,128)(2,1)S(1)}, bf16[1024,512]{1,0:T(8,128)(2,1)S(1)}, u32[]{:S(2)}, u32[]{:S(2)}) %collective-permute-start.26) | collective-permute-done | bytes 1048608 | tf_op jit(solution)/shard_map/ppermute | solution.py:33
  (76 shorter events, 35.7 us)
Async XLA Ops:
  6.5 113.5 %all-gather.2.cloned.1.call-start = ((), (), s32[]{:S(2)}) async-start(), calls=%async_computation | async-start | bytes 8650752 | tf_op jit(solution)/shard_map/all_gather | solution.py:192
  6.5 17.0 %collective-permute-start.21 = (bf16[64,512]{1,0:T(8,128)(2,1)}, bf16[64,512]{1,0:T(8,128)(2,1)S(1)}, u32[]{:S(2)}, u32[]{:S(2)}) collective-permute-start(bf16[64,512]{1,0:T(8,128)(2,1)} %param.7), channel_id=1, source_target_pairs={{0,4},{1,5},{2,6},{3,7},{4,0},{5,1},{6,2},{7,3},{8,12},{9,13},{10,... | collective-permute-start | bytes 196616 | tf_op jit(solution)/shard_map/ppermute | solution.py:178
  12.0 11.6 %collective-permute-start.23 = (bf16[64,512]{1,0:T(8,128)(2,1)}, bf16[64,512]{1,0:T(8,128)(2,1)S(1)}, u32[]{:S(2)}, u32[]{:S(2)}) collective-permute-start(bf16[64,512]{1,0:T(8,128)(2,1)} %param.7), channel_id=1, source_target_pairs={{0,260},{1,261},{2,262},{3,263},{4,256},{5,257},{6,258},{7,259},{2... | collective-permute-start | bytes 196616 | tf_op jit(solution)/shard_map/ppermute | solution.py:180
  15.3 15.1 %collective-permute-start.22 = (bf16[64,512]{1,0:T(8,128)(2,1)}, bf16[64,512]{1,0:T(8,128)(2,1)S(1)}, u32[]{:S(2)}, u32[]{:S(2)}) collective-permute-start(bf16[64,512]{1,0:T(8,128)(2,1)} %param.7), channel_id=1, source_target_pairs={{0,256},{256,0},{1,257},{257,1},{2,258},{258,2},{3,259},{259,3},{4... | collective-permute-start | bytes 196616 | tf_op jit(solution)/shard_map/ppermute | solution.py:175
  33.2 22.9 %collective-permute-start = (bf16[3,144,512]{2,1,0:T(8,128)(2,1)S(1)}, bf16[3,144,512]{2,1,0:T(8,128)(2,1)S(1)}, u32[]{:S(2)}, u32[]{:S(2)}) collective-permute-start(bf16[3,144,512]{2,1,0:T(8,128)(2,1)S(1)} %get-tuple-element.6), channel_id=1, source_target_pairs={{0,8},{8,16},{16,24},{24,32},{32,40},{40,48},{48,56},{56,64},{64,7... | collective-permute-start | bytes 1327112 | tf_op jit(solution)/shard_map/ppermute | solution.py:177
  42.4 36.3 %collective-permute-start.2 = (bf16[512,512]{1,0:T(8,128)(2,1)S(1)}, bf16[512,512]{1,0:T(8,128)(2,1)S(1)}, u32[]{:S(2)}, u32[]{:S(2)}) collective-permute-start(bf16[512,512]{1,0:T(8,128)(2,1)S(1)} %late_tokens.1.refs_1_), channel_id=1, source_target_pairs={{1,0},{2,1},{3,2},{4,3},{5,4},{6,5},{7,6},{14,15},{13,14},{12,13},... | collective-permute-start | bytes 1572872 | tf_op jit(solution)/shard_map/ppermute | solution.py:25
  60.2 30.4 %collective-permute-start.1 = (bf16[512,512]{1,0:T(8,128)(2,1)S(1)}, bf16[512,512]{1,0:T(8,128)(2,1)S(1)}, u32[]{:S(2)}, u32[]{:S(2)}) collective-permute-start(bf16[512,512]{1,0:T(8,128)(2,1)S(1)} %early_tokens.1.refs_0_), channel_id=1, source_target_pairs={{1,0},{2,1},{3,2},{4,3},{5,4},{6,5},{7,6},{14,15},{13,14},{12,13},... | collective-permute-start | bytes 1572872 | tf_op jit(solution)/shard_map/ppermute | solution.py:25
  78.7 14.0 %collective-permute-start.4 = (bf16[512,512]{1,0:T(8,128)(2,1)S(1)}, bf16[512,512]{1,0:T(8,128)(2,1)S(1)}, u32[]{:S(2)}, u32[]{:S(2)}) collective-permute-start(bf16[512,512]{1,0:T(8,128)(2,1)S(1)} %collective-permute-done.2.refs_3_), channel_id=1, source_target_pairs={{1,0},{2,1},{3,2},{4,3},{5,4},{6,5},{14,15},{13,14},{12,13},{11,12... | collective-permute-start | bytes 1572872 | tf_op jit(solution)/shard_map/ppermute | solution.py:25
  91.3 5.9 %collective-permute-start.14 = (bf16[512,512]{1,0:T(8,128)(2,1)S(1)}, bf16[512,512]{1,0:T(8,128)(2,1)}, u32[]{:S(2)}, u32[]{:S(2)}) collective-permute-start(bf16[512,512]{1,0:T(8,128)(2,1)S(1)} %late_tokens.1.refs_1_), channel_id=1, source_target_pairs={{0,1},{1,2},{2,3},{15,14},{14,13},{13,12},{16,17},{17,18},{18,19},... | collective-permute-start | bytes 1572872 | tf_op jit(solution)/shard_map/ppermute | solution.py:29
  92.8 5.9 %collective-permute-start.6 = (bf16[512,512]{1,0:T(8,128)(2,1)S(1)}, bf16[512,512]{1,0:T(8,128)(2,1)S(1)}, u32[]{:S(2)}, u32[]{:S(2)}) collective-permute-start(bf16[512,512]{1,0:T(8,128)(2,1)S(1)} %collective-permute-done.4.refs_5_), channel_id=1, source_target_pairs={{1,0},{2,1},{3,2},{4,3},{5,4},{14,15},{13,14},{12,13},{11,12},{10,... | collective-permute-start | bytes 1572872 | tf_op jit(solution)/shard_map/ppermute | solution.py:25
  93.5 6.7 %collective-permute-start.5 = (bf16[512,512]{1,0:T(8,128)(2,1)S(1)}, bf16[512,512]{1,0:T(8,128)(2,1)}, u32[]{:S(2)}, u32[]{:S(2)}) collective-permute-start(bf16[512,512]{1,0:T(8,128)(2,1)S(1)} %collective-permute-done.3.refs_4_), channel_id=1, source_target_pairs={{1,0},{2,1},{3,2},{4,3},{5,4},{14,15},{13,14},{12,13},{11,12},{10,... | collective-permute-start | bytes 1572872 | tf_op jit(solution)/shard_map/ppermute | solution.py:25
  97.2 5.9 %collective-permute-start.15 = (bf16[512,512]{1,0:T(8,128)(2,1)}, bf16[512,512]{1,0:T(8,128)(2,1)}, u32[]{:S(2)}, u32[]{:S(2)}) collective-permute-start(bf16[512,512]{1,0:T(8,128)(2,1)} %collective-permute-done.14.refs_13_), channel_id=1, source_target_pairs={{1,2},{2,3},{14,13},{13,12},{17,18},{18,19},{30,29},{29,28},{33,34... | collective-permute-start | bytes 1572872 | tf_op jit(solution)/shard_map/ppermute | solution.py:29
  98.7 5.9 %collective-permute-start.8 = (bf16[512,512]{1,0:T(8,128)(2,1)S(1)}, bf16[512,512]{1,0:T(8,128)(2,1)}, u32[]{:S(2)}, u32[]{:S(2)}) collective-permute-start(bf16[512,512]{1,0:T(8,128)(2,1)S(1)} %collective-permute-done.6.refs_7_), channel_id=1, source_target_pairs={{1,0},{2,1},{3,2},{4,3},{14,15},{13,14},{12,13},{11,12},{17,16},{1... | collective-permute-start | bytes 1572872 | tf_op jit(solution)/shard_map/ppermute | solution.py:25
  100.1 5.9 %collective-permute-start.7 = (bf16[512,512]{1,0:T(8,128)(2,1)}, bf16[512,512]{1,0:T(8,128)(2,1)}, u32[]{:S(2)}, u32[]{:S(2)}) collective-permute-start(bf16[512,512]{1,0:T(8,128)(2,1)} %collective-permute-done.5.refs_6_), channel_id=1, source_target_pairs={{1,0},{2,1},{3,2},{4,3},{14,15},{13,14},{12,13},{11,12},{17,16},{1... | collective-permute-start | bytes 1572872 | tf_op jit(solution)/shard_map/ppermute | solution.py:25
  101.6 6.1 %collective-permute-start.11 = (bf16[512,512]{1,0:T(8,128)(2,1)}, bf16[512,512]{1,0:T(8,128)(2,1)}, u32[]{:S(2)}, u32[]{:S(2)}) collective-permute-start(bf16[512,512]{1,0:T(8,128)(2,1)} %collective-permute-done.10.refs_12_), channel_id=1, source_target_pairs={{1,2},{2,3},{14,13},{13,12},{17,18},{18,19},{30,29},{29,28},{33,34... | collective-permute-start | bytes 1572872 | tf_op jit(solution)/shard_map/ppermute | solution.py:29
  103.1 9.1 %collective-permute-start.16 = (bf16[512,512]{1,0:T(8,128)(2,1)}, bf16[512,512]{1,0:T(8,128)(2,1)}, u32[]{:S(2)}, u32[]{:S(2)}) collective-permute-start(bf16[512,512]{1,0:T(8,128)(2,1)} %collective-permute-done.15.refs_15_), channel_id=1, source_target_pairs={{2,3},{13,12},{18,19},{29,28},{34,35},{45,44},{50,51},{61,60},{66,... | collective-permute-start | bytes 1572872 | tf_op jit(solution)/shard_map/ppermute | solution.py:29
  107.7 6.4 %collective-permute-start.12 = (bf16[512,512]{1,0:T(8,128)(2,1)}, bf16[512,512]{1,0:T(8,128)(2,1)}, u32[]{:S(2)}, u32[]{:S(2)}) collective-permute-start(bf16[512,512]{1,0:T(8,128)(2,1)} %collective-permute-done.11.refs_14_), channel_id=1, source_target_pairs={{2,3},{13,12},{18,19},{29,28},{34,35},{45,44},{50,51},{61,60},{66,... | collective-permute-start | bytes 1572872 | tf_op jit(solution)/shard_map/ppermute | solution.py:29
  109.3 5.9 %collective-permute-start.18 = (bf16[512,512]{1,0:T(8,128)(2,1)}, bf16[512,512]{1,0:T(8,128)(2,1)}, u32[]{:S(2)}, u32[]{:S(2)}) collective-permute-start(bf16[512,512]{1,0:T(8,128)(2,1)} %collective-permute-done.13), channel_id=1, source_target_pairs={{1,0},{2,1},{14,15},{13,14},{17,16},{18,17},{30,31},{29,30},{33,32... | collective-permute-start | bytes 1572872 | tf_op jit(solution)/shard_map/ppermute | solution.py:25
  110.7 6.0 %collective-permute-start.17 = (bf16[512,512]{1,0:T(8,128)(2,1)}, bf16[512,512]{1,0:T(8,128)(2,1)}, u32[]{:S(2)}, u32[]{:S(2)}) collective-permute-start(bf16[512,512]{1,0:T(8,128)(2,1)} %collective-permute-done.9), channel_id=1, source_target_pairs={{1,0},{2,1},{14,15},{13,14},{17,16},{18,17},{30,31},{29,30},{33,32... | collective-permute-start | bytes 1572872 | tf_op jit(solution)/shard_map/ppermute | solution.py:25
  115.2 23.4 %collective-permute-start.20 = (bf16[512,512]{1,0:T(8,128)(2,1)}, bf16[512,512]{1,0:T(8,128)(2,1)}, u32[]{:S(2)}, u32[]{:S(2)}) collective-permute-start(bf16[512,512]{1,0:T(8,128)(2,1)} %collective-permute-done.18.refs_1_), channel_id=1, source_target_pairs={{1,0},{14,15},{17,16},{30,31},{33,32},{46,47},{49,48},{62,63},{65,... | collective-permute-start | bytes 1572872 | tf_op jit(solution)/shard_map/ppermute | solution.py:25
  116.7 21.9 %collective-permute-start.19 = (bf16[512,512]{1,0:T(8,128)(2,1)}, bf16[512,512]{1,0:T(8,128)(2,1)}, u32[]{:S(2)}, u32[]{:S(2)}) collective-permute-start(bf16[512,512]{1,0:T(8,128)(2,1)} %collective-permute-done.17.refs_0_), channel_id=1, source_target_pairs={{1,0},{14,15},{17,16},{30,31},{33,32},{46,47},{49,48},{62,63},{65,... | collective-permute-start | bytes 1572872 | tf_op jit(solution)/shard_map/ppermute | solution.py:25
  137.8 21.7 %collective-permute-start.25 = (bf16[1024,512]{1,0:T(8,128)(2,1)S(1)}, bf16[1024,512]{1,0:T(8,128)(2,1)S(1)}, u32[]{:S(2)}, u32[]{:S(2)}) collective-permute-start(bf16[1024,512]{1,0:T(8,128)(2,1)S(1)} %convert_element_type.22), channel_id=1, source_target_pairs={{1,5},{14,10},{17,21},{30,26},{33,37},{46,42},{49,53},{62,58},{65,... | collective-permute-start | bytes 3145736 | tf_op jit(solution)/shard_map/ppermute | solution.py:33
  140.7 18.9 %collective-permute-start.24 = (bf16[1024,512]{1,0:T(8,128)(2,1)S(1)}, bf16[1024,512]{1,0:T(8,128)(2,1)S(1)}, u32[]{:S(2)}, u32[]{:S(2)}) collective-permute-start(bf16[1024,512]{1,0:T(8,128)(2,1)S(1)} %partner_last.1), channel_id=1, source_target_pairs={{0,4},{15,11},{16,20},{31,27},{32,36},{47,43},{48,52},{63,59},{64,... | collective-permute-start | bytes 3145736 | tf_op jit(solution)/shard_map/ppermute | solution.py:33
  141.6 85.8 %collective-permute-start.26 = (bf16[1024,512]{1,0:T(8,128)(2,1)S(1)}, bf16[1024,512]{1,0:T(8,128)(2,1)S(1)}, u32[]{:S(2)}, u32[]{:S(2)}) collective-permute-start(bf16[1024,512]{1,0:T(8,128)(2,1)S(1)} %convert_element_type.23), channel_id=1, source_target_pairs={{2,6},{3,7},{13,9},{12,8},{18,22},{19,23},{29,25},{28,24},{34,38},... | collective-permute-start | bytes 3145736 | tf_op jit(solution)/shard_map/ppermute | solution.py:33
  (14 other events, 58.1 us)
Sparse Core Ops, SparseCore 0:
  32.1 69.9 all-gather.1

commit v2 on v0

v2 whole, which is shorter than its diff:
```python
import functools

import jax
import jax.numpy as jnp
from jax import lax
from jax.experimental import pallas as pl
from jax.experimental.pallas import tpu as pltpu
from jax.sharding import Mesh, PartitionSpec as P

SEQ = ("zh", "y", "x", "c")
PLANE = ("y", "x", "c")
TP = ("th", "tl")
LINE = ("c",) + TP
LANES = 128
LINE_LEN = 8
WORKERS = 4
VMEM = 60 << 20


def on_line(pairs):
    place = lambda u, core: core * LINE_LEN + (u if core == 0 else LINE_LEN - 1 - u)
    return [(place(a, core), place(b, core)) for core in (0, 1) for a, b in pairs]


def inward(block, step):
    return lax.ppermute(block, LINE, on_line([(u, u - 1) for u in range(1, LINE_LEN + 1 - step)]))


def outward(block, step):
    return lax.ppermute(block, LINE, on_line([(u, u + 1) for u in range(step - 1, WORKERS - 1)]))


def deliver(block, workers):
    return lax.ppermute(block, LINE, on_line([(u, u + WORKERS) for u in workers]))


def feature(rows, taps):
    return (
        taps[0:1] * rows
        + taps[1:2] * pltpu.roll(rows, 1, 0)
        + taps[2:3] * pltpu.roll(rows, 2, 0)
    )


def toeplitz(filt_ref, toep):
    groups, taps = filt_ref.shape[1], filt_ref.shape[2]
    lag = lax.broadcasted_iota(jnp.int32, (taps, 2 * taps), 0)
    col = lax.broadcasted_iota(jnp.int32, (taps, 2 * taps), 1)
    flip = jnp.where(lag + col == taps, 1.0, 0.0).astype(jnp.bfloat16)
    first = jnp.dot(filt_ref[0], flip, preferred_element_type=jnp.float32)
    for g in range(groups):
        wide = jnp.broadcast_to(first[g : g + 1], (taps, 2 * taps))
        wide = pltpu.roll(wide, 0, 1, stride=1, stride_axis=0)
        toep[g * taps : (g + 1) * taps] = wide.astype(jnp.bfloat16)


def convolve(gated, query, groups, taps, toep, out_ref):
    group_of = lax.broadcasted_iota(jnp.int32, (taps, 2 * LANES), 1) % LANES // (LANES // groups)
    for pair in range(query.shape[0] // taps // 2):
        base = 2 * pair * taps
        window = jnp.concatenate(
            [gated[base : base + 2 * taps], gated[base + taps : base + 3 * taps]], axis=1
        )
        every = jnp.dot(toep[...], window, preferred_element_type=jnp.float32)
        conv = every[:taps]
        for g in range(1, groups):
            conv = jnp.where(group_of == g, every[g * taps : (g + 1) * taps], conv)
        for k in range(2):
            at = base + k * taps
            piece = conv[:, k * LANES : (k + 1) * LANES] * query[at : at + taps]
            out_ref[at : at + taps] = piece.astype(jnp.bfloat16)


def tail_kernel(x_ref, taps_ref, tail_ref):
    taps = tail_ref.shape[0] - 32
    rows = [x_ref[s, x_ref.shape[1] - taps - 16 :].astype(jnp.float32) for s in range(3)]
    gated = feature(rows[1], taps_ref[1]) * feature(rows[2], taps_ref[2])
    raw = [r[taps + 8 :] for r in rows]
    raw.append(jnp.zeros((8, LANES), jnp.float32))
    tail_ref[:taps] = gated[16:].astype(jnp.bfloat16)
    tail_ref[taps:] = jnp.concatenate(raw, axis=0).astype(jnp.bfloat16)


def late_kernel(x_ref, taps_ref, filt_ref, out_ref, toep):
    groups, taps = filt_ref.shape[1], filt_ref.shape[2]
    toeplitz(filt_ref, toep)
    rows = [x_ref[s, out_ref.shape[0] - taps - 16 :].astype(jnp.float32) for s in range(3)]
    query = feature(rows[0], taps_ref[0])[taps + 16 :]
    gated = feature(rows[1], taps_ref[1]) * feature(rows[2], taps_ref[2])
    convolve(gated[16:].astype(jnp.bfloat16), query, groups, taps, toep, out_ref)


def early_kernel(x_ref, halo_ref, taps_ref, filt_ref, out_ref, toep):
    groups, taps = filt_ref.shape[1], filt_ref.shape[2]
    half = out_ref.shape[0]
    toeplitz(filt_ref, toep)
    before = halo_ref[taps:].astype(jnp.float32)

    def featured(s):
        own = x_ref[s, :half].astype(jnp.float32)
        rows = jnp.concatenate([before[8 * s : 8 * s + 8], own], axis=0)
        return feature(rows, taps_ref[s])[8:]

    gated = (featured(1) * featured(2)).astype(jnp.bfloat16)
    gated = jnp.concatenate([halo_ref[:taps], gated], axis=0)
    convolve(gated, featured(0), groups, taps, toep, out_ref)


def lane_tiles(rows):
    return pl.BlockSpec((rows, LANES), lambda i: (0, i))


LOCAL = dict(
    compiler_params=pltpu.CompilerParams(vmem_limit_bytes=VMEM),
    cost_estimate=pl.CostEstimate(flops=1 << 30, bytes_accessed=4 << 20, transcendentals=0),
)


def local_tail(x, short_taps, taps):
    streams, tokens, channels = x.shape
    last = 2 * taps
    return pl.pallas_call(
        tail_kernel,
        grid=(channels // LANES,),
        in_specs=[
            pl.BlockSpec((streams, last, LANES), lambda i: (0, tokens // last - 1, i)),
            pl.BlockSpec((streams, 3, LANES), lambda i: (0, 0, i)),
        ],
        out_specs=lane_tiles(taps + 32),
        out_shape=jax.ShapeDtypeStruct((taps + 32, channels), jnp.bfloat16),
        name="tail_tokens",
        **LOCAL,
    )(x, short_taps)


def local_part(x, halo, short_taps, long_filter):
    streams, tokens, channels = x.shape
    groups, taps = long_filter.shape
    tiles = channels // LANES
    filt = long_filter.reshape(tiles, groups // tiles, taps)
    in_specs = [
        pl.BlockSpec((streams, tokens, LANES), lambda i: (0, 0, i)),
        pl.BlockSpec((streams, 3, LANES), lambda i: (0, 0, i)),
        pl.BlockSpec((1, groups // tiles, taps), lambda i: (i, 0, 0)),
    ]
    operands = [x, short_taps, filt]
    if halo is not None:
        in_specs.insert(1, lane_tiles(halo.shape[0]))
        operands.insert(1, halo)
    return pl.pallas_call(
        late_kernel if halo is None else early_kernel,
        grid=(tiles,),
        in_specs=in_specs,
        out_specs=lane_tiles(tokens // 2),
        out_shape=jax.ShapeDtypeStruct((tokens // 2, channels), jnp.bfloat16),
        scratch_shapes=[pltpu.VMEM((groups // tiles * taps, 2 * taps), jnp.bfloat16)],
        name="late_tokens" if halo is None else "early_tokens",
        **LOCAL,
    )(*operands)


def project_kernel(slots, side, outs, has_start, place_ref, *refs):
    total = sum(count for _, options in slots for _, count in options)
    x_refs, w_ref = refs[:total], refs[total]
    held, weight, acc, x_sems, w_sems, start_sem = refs[-6:]
    out_refs = refs[len(refs) - 6 - outs : len(refs) - 6]
    at, toward, th, u = [place_ref[i] for i in range(4)]
    parts, half, depth = held.shape[1:]
    per_zh = w_ref.shape[0]

    def fetch(slot, first, count, part):
        source = x_refs[first + part] if count > 1 else x_refs[first].at[pl.ds(part * half, half)]
        return pltpu.make_async_copy(source, held.at[slot, part], x_sems.at[slot, part])

    def rows(slot, y, z):
        return pltpu.make_async_copy(w_ref.at[y, :, z], weight.at[slot], w_sems.at[slot])

    firsts = []
    position = 0
    for slot, (limit, options) in enumerate(slots):
        distance = options[0][0]
        if limit is not None:
            distance = jnp.where(u < limit, distance, options[1][0])
        block = jnp.clip(at + toward * distance, 0, LINE_LEN - 1)
        upper = jnp.where(block >= per_zh, 1, 0)
        column = th if side == 0 else 1 - th
        rows(slot, block - per_zh * upper, 2 * upper + column).start()
        firsts.append((position, options[0][1]))
        for option, (_, count) in enumerate(options):
            for part in range(parts):
                copy = fetch(slot, position, count, part)
                if limit is None:
                    copy.start()
                else:
                    pl.when(u < limit if option == 0 else u >= limit)(copy.start)
            position += count
    if has_start:
        from_start = pltpu.make_async_copy(refs[total + 1], acc, start_sem)
        from_start.start()
        from_start.wait()

    for slot in range(len(slots)):
        rows(slot, 0, 0).wait()
        for part in range(parts):
            fetch(slot, *firsts[slot], part).wait()
        term = jnp.dot(
            held[slot].reshape(parts * half, depth),
            weight[slot].reshape(depth, weight.shape[-1]),
            preferred_element_type=jnp.float32,
        )
        if slot > 0 or has_start:
            term = acc[...] + term
        if slot < len(slots) - 1:
            acc[...] = term
        else:
            for out_ref in out_refs:
                out_ref[...] = term.astype(out_ref.dtype)


def project(slots, place, weights, side, start, kinds, name):
    half, depth = slots[0][1][0][1][0].shape
    ys, members, zs, rows, columns = weights.shape
    blocks, tokens = len(slots), 2 * half
    operands = [part for _, options in slots for _, block in options for part in block] + [weights]
    if start is not None:
        operands.append(start)
    shape_of_slots = tuple(
        (limit, tuple((distance, len(block)) for distance, block in options)) for limit, options in slots
    )
    return pl.pallas_call(
        functools.partial(project_kernel, shape_of_slots, side, len(kinds), start is not None),
        grid_spec=pltpu.PrefetchScalarGridSpec(
            num_scalar_prefetch=1,
            grid=(1,),
            in_specs=[pl.BlockSpec(memory_space=pl.ANY)] * len(operands),
            out_specs=[pl.BlockSpec((tokens, columns), lambda i, place: (0, 0))] * len(kinds),
            scratch_shapes=[
                pltpu.VMEM((blocks, 2, half, depth), jnp.bfloat16),
                pltpu.VMEM((blocks, members, rows, columns), jnp.bfloat16),
                pltpu.VMEM((tokens, columns), jnp.float32),
                pltpu.SemaphoreType.DMA((blocks, 2)),
                pltpu.SemaphoreType.DMA((blocks,)),
                pltpu.SemaphoreType.DMA,
            ],
        ),
        out_shape=[jax.ShapeDtypeStruct((tokens, columns), kind) for kind in kinds],
        compiler_params=pltpu.CompilerParams(vmem_limit_bytes=VMEM),
        cost_estimate=pl.CostEstimate(
            flops=tokens * columns, bytes_accessed=tokens * columns, transcendentals=0
        ),
        name=name,
    )(place, *operands)


def per_device(projected, short_taps, long_filter, out_weight):
    core, at, th = lax.axis_index("c"), lax.axis_index(TP), lax.axis_index("th")
    u = jnp.where(core == 0, at, LINE_LEN - 1 - at)
    toward = jnp.where(core == 0, 1, -1)
    place = jnp.stack([at, toward, th, u]).astype(jnp.int32)
    in_order = lax.optimization_barrier

    tail = local_tail(projected, short_taps, long_filter.shape[1])
    next_seq = [(i, i + 1) for i in range(lax.axis_size(SEQ) - 1)]
    halo = lax.ppermute(tail, SEQ, next_seq)

    projected, place, _ = in_order((projected, place, tail))
    late = local_part(projected, None, short_taps, long_filter)

    own_shard, _ = in_order((out_weight, late))
    shard = lax.all_gather(own_shard, ("zh", "th"), axis=0, tiled=True)
    projected, halo, shard = in_order((projected, halo, shard))
    weights = lax.all_gather(shard, PLANE, axis=0, tiled=True)
    projected, halo, _ = in_order((projected, halo, shard))
    early = local_part(projected, halo, short_taps, long_filter)
    rows, columns = out_weight.shape
    parts = lax.axis_size(("zh", "th"))
    weights = weights.reshape(lax.axis_size("y"), -1, parts, rows, columns)

    came = [(early, late)]
    back = [(early, late)]
    for step in range(1, LINE_LEN - 2):
        before, behind = came[-1]
        before = inward(before, step)
        behind = inward(behind, step)
        came.append((before, behind))
        if step > 2:
            back.append(tuple(outward(part, step - 2) for part in back[-1]))

    kinds = (jnp.float32, jnp.bfloat16)
    near = [(None, [(d, came[d])]) for d in range(5)]
    (total,) = project(near, place, weights, 1, None, kinds[:1], "partner_near")
    fifth = came[5]
    came.append(tuple(inward(part, LINE_LEN - 2) for part in fifth))
    sixth, total = in_order((came[6], total))
    came.append(tuple(inward(part, LINE_LEN - 1) for part in sixth))
    far = [(3, [(5, fifth), (-3, back[3])]), (None, [(-2, back[2])]), (None, [(-1, back[1])])]
    total, ready = project(far, place, weights, 1, total, kinds, "partner_far")
    sent_two = deliver(ready, (2, 3))
    last, total = in_order((came[7], total))
    end = [(None, [(6, sixth)]), (None, [(7, last)])]
    (ready,) = project(end, place, weights, 1, total, kinds[1:], "partner_last")
    sent_last = deliver(ready, (0, 1))

    every = near + far[:1] + [(2, [(6, sixth), (-2, back[2])]), (1, [(7, last), (-1, back[1])])]
    (mine,) = project(every, place, weights, 0, None, kinds[1:], "own_columns")
    given = jnp.where(u < WORKERS + 2, sent_last, sent_two)
    return jnp.where(u < WORKERS, mine, given)


def solution(mesh):
    split = Mesh(mesh.devices.reshape(2, 4, 4, 2, 2, WORKERS), SEQ + TP)
    in_specs = (P(None, SEQ, TP), P(None, None, TP), P(TP, None), P(SEQ, TP))
    return jax.shard_map(
        per_device, mesh=split, in_specs=in_specs, out_specs=P(SEQ, TP), check_vma=False
    )
```

time: 346 us -> 200 us (0.58); the launches traced: 346 us -> 196 us
  waiting for transfers between devices: 286 us -> 78.6 us
  Pallas kernels: 0 us -> 44.2 us
  blocking collectives: 0 us -> 26.9 us
  starting transfers between devices: 6.64 us -> 29.8 us
  matrix products: 19.1 us -> 0 us
  local copies, waits for them, and re-layouts: 10.2 us -> 1.04 us
  other arithmetic: 10.3 us -> 1.73 us
    all_gather x2 -> x1, waiting for transfers between devices: 282 us -> 35.6 us  [per_device(): weights = lax.all_gather(shard, PLANE, axis=0, tiled=True)]
    pallas_call x0 -> x7, Pallas kernels: none -> 44.2 us  [the longest x4 30 us: project(): pl.pallas_call(functools.partial(project_kernel, shape_of_slots, side, le...]
    ppermute x2 -> x23, waiting for transfers between devices: 3.37 us -> 43 us  [the longest x2 37.3 us: deliver(): lax.ppermute(block, LINE, on_line([(u, u + WORKERS) for u in workers]))]
    all_gather x0 -> x1, blocking collectives: none -> 26.9 us  [per_device(): shard = lax.all_gather(own_shard, ('zh', 'th'), axis=0, tiled=True)]
    ppermute x2 -> x23, starting transfers between devices: 6.6 us -> 29.8 us  [the longest x14 16.8 us: inward(): lax.ppermute(block, LINE, on_line([(u, u - 1) for u in range(1, LINE_LEN...]
    dot_general x3 -> x0, matrix products: 19.1 us -> none  [the longest x1 10.1 us: per_device(): jnp.dot(whole, lax.all_gather(out_weight, 'seq', axis=0, tiled=True), pre...]
    add x2 -> x0, other arithmetic: 4.77 us -> none  [the longest x1 4.77 us: featurize(): tap_zero * extended[:, 2:] + tap_one * extended[:, 1:-1]]
    unnamed x9 -> x32, local copies, waits for them, and re-layouts: 5.55 us -> 1.04 us
  transfers between devices with their start and end apart: 4 -> 24, of which waited for: 3 -> 3; matrix products, arithmetic and copies ran while one was open for 8% -> 0% of each run, Pallas kernels for 0% -> 21%
where the time goes in v2:
time: 200 us; the launch traced here: 196 us
  waiting for transfers between devices  78.6 us (39%)
  Pallas kernels  44.2 us (22%)
  starting transfers between devices  29.8 us (15%)
  blocking collectives  26.9 us (13%)
  between operations  13.8 us (7%)
    ppermute x2, waiting for transfers between devices, deliver(): lax.ppermute(block, LINE, on_line([(u, u + WORKERS) for u in workers]))  37.3 us
    all_gather x1, waiting for transfers between devices, per_device(): weights = lax.all_gather(shard, PLANE, axis=0, tiled=True)  35.6 us
    pallas_call x4, Pallas kernels, project(): pl.pallas_call(functools.partial(project_kernel, shape_of_slots, side, le...  30 us
    all_gather x1, blocking collectives, per_device(): shard = lax.all_gather(own_shard, ('zh', 'th'), axis=0, tiled=True)  26.9 us
    ppermute x14, starting transfers between devices, inward(): lax.ppermute(block, LINE, on_line([(u, u - 1) for u in range(1, LINE_LEN...  16.8 us
    pallas_call x2, Pallas kernels, local_part(): pl.pallas_call(late_kernel if halo is None else early_kernel, grid=(tiles...  11 us
    ppermute x6, starting transfers between devices, outward(): lax.ppermute(block, LINE, on_line([(u, u + 1) for u in range(step - 1, WO...  6.45 us
    ppermute x14, waiting for transfers between devices, inward(): lax.ppermute(block, LINE, on_line([(u, u - 1) for u in range(1, LINE_LEN...  5.7 us
  transfers between devices with their start and end apart: 24, of which 3 were waited for; matrix products, arithmetic and copies ran while one was open for 0% of the time, Pallas kernels for 21%

profile of v2, /device:TPU:1, one launch (start us, length us, event | category | flops | bytes accessed | tf_op | source)
XLA Modules:
  0.0 196.2 jit_solution(7186935156187430478)
XLA Ops:
  6.5 3.3 %tail_tokens.1 = bf16[160,512]{1,0:T(8,128)(2,1)} custom-call(bf16[3,1024,512]{2,1,0:T(8,128)(2,1)} %x_ref.3, f32[3,3,512]{2,1,0:T(4,128)} %taps_ref.5), custom_call_target="tpu_custom_call" | custom-call | flops 1073741824 | bytes 4194304 | tf_op jit(solution)/shard_map/tail_tokens/pallas_call | solution.py:122
  9.8 4.5 %collective-permute-start = (bf16[160,512]{1,0:T(8,128)(2,1)}, bf16[160,512]{1,0:T(8,128)(2,1)S(1)}, u32[]{:S(2)}, u32[]{:S(2)}) collective-permute-start(bf16[160,512]{1,0:T(8,128)(2,1)} %tail_tokens.1), channel_id=1, source_target_pairs={{0,8},{8,16},{16,24},{24,32},{32,40},{40,48},{48,56},{56,64},{64,7... | collective-permute-start | bytes 491528 | tf_op jit(solution)/shard_map/ppermute | solution.py:264
  15.0 5.6 %late_tokens.1.refs_1_ = bf16[512,512]{1,0:T(8,128)(2,1)} custom-call(bf16[3,1024,512]{2,1,0:T(8,128)(2,1)} %x_ref.3, f32[3,3,512]{2,1,0:T(4,128)} %taps_ref.5, bf16[4,8,128]{2,1,0:T(8,128)(2,1)} %bitcast.10), custom_call_target="tpu_custom_call" | custom-call | flops 1073741824 | bytes 4194304 | tf_op jit(solution)/shard_map/late_tokens/pallas_call | solution.py:150
  20.5 26.9 %all_gather.6 = bf16[256,512]{1,0:T(8,128)(2,1)} all-gather(bf16[64,512]{1,0:T(8,128)(2,1)S(1)} %copy-done.14), channel_id=1, replica_groups=mesh['zh'=2,'y'=4,'x'=4,'c'=2,'th'=2,'tl'=4] {'zh','th'}, dimensions={0}, use_global_device_ids=true | all-gather | bytes 327680 | tf_op jit(solution)/shard_map/all_gather | solution.py:270
  47.5 2.8 %collective-permute-start.2 = (bf16[512,512]{1,0:T(8,128)(2,1)}, bf16[512,512]{1,0:T(8,128)(2,1)S(1)}, u32[]{:S(2)}, u32[]{:S(2)}) collective-permute-start(bf16[512,512]{1,0:T(8,128)(2,1)} %late_tokens.1.refs_1_), channel_id=1, source_target_pairs={{1,0},{2,1},{3,2},{4,3},{5,4},{6,5},{7,6},{14,15},{13,14},{12,13},... | collective-permute-start | bytes 1572872 | tf_op jit(solution)/shard_map/ppermute | solution.py:26
  50.2 5.4 %early_tokens.1.refs_0_ = bf16[512,512]{1,0:T(8,128)(2,1)} custom-call(bf16[3,1024,512]{2,1,0:T(8,128)(2,1)} %x_ref.3, bf16[160,512]{1,0:T(8,128)(2,1)} %copy-done.15, f32[3,3,512]{2,1,0:T(4,128)} %taps_ref.5, bf16[4,8,128]{2,1,0:T(8,128)(2,1)} %bitcast.11), custom_call_target="tpu_custom_call" | custom-call | flops 1073741824 | bytes 4194304 | tf_op jit(solution)/shard_map/early_tokens/pallas_call | solution.py:150
  55.7 2.6 %collective-permute-start.1 = (bf16[512,512]{1,0:T(8,128)(2,1)}, bf16[512,512]{1,0:T(8,128)(2,1)S(1)}, u32[]{:S(2)}, u32[]{:S(2)}) collective-permute-start(bf16[512,512]{1,0:T(8,128)(2,1)} %early_tokens.1.refs_0_), channel_id=1, source_target_pairs={{1,0},{2,1},{3,2},{4,3},{5,4},{6,5},{7,6},{14,15},{13,14},{12,13},... | collective-permute-start | bytes 1572872 | tf_op jit(solution)/shard_map/ppermute | solution.py:26
  59.0 5.7 %collective-permute-done.1.refs_2_ = bf16[512,512]{1,0:T(8,128)(2,1)S(1)} collective-permute-done((bf16[512,512]{1,0:T(8,128)(2,1)}, bf16[512,512]{1,0:T(8,128)(2,1)S(1)}, u32[]{:S(2)}, u32[]{:S(2)}) %collective-permute-start.1) | collective-permute-done | bytes 524320 | tf_op jit(solution)/shard_map/ppermute | solution.py:26
  69.7 1.5 collective-permute-start.10
  71.2 1.5 collective-permute-start.9
  73.4 1.5 collective-permute-start.12
  74.9 1.5 collective-permute-start.18
  76.3 1.5 collective-permute-start.17
  77.8 1.5 collective-permute-start.16
  79.3 1.5 collective-permute-start.13
  80.7 35.6 %all-gather.2.cloned.1.call-done = bf16[8192,512]{1,0:T(8,128)(2,1)} async-done(((bf16[256,512]{1,0:T(8,128)(2,1)}), bf16[8192,512]{1,0:T(8,128)(2,1)}) %all-gather.2.cloned.1.call-update) | async-done | bytes 8388624 | tf_op jit(solution)/shard_map/all_gather | solution.py:272
  116.4 7.2 %partner_near.1.refs_9_ = f32[1024,512]{1,0:T(8,128)} custom-call(s32[4]{0:T(128)} %pad_add_fusion.place_ref, bf16[512,512]{1,0:T(8,128)(2,1)} %early_tokens.1.refs_0_, bf16[512,512]{1,0:T(8,128)(2,1)} %late_tokens.1.refs_1_, bf16[512,512]{1,0:T(8,128)(2,1)} %copy-done.2, bf16[512,512]{1,0:T(8,128)(2,1)} %copy-done.1, bf16[512,512]{1,0:T(8,128)(2,1)} %copy-done.4, ...), custom_call_target="tpu_custom_call" | custom-call | flops 524288 | bytes 524288 | tf_op jit(solution)/shard_map/partner_near/pallas_call | solution.py:230
  125.1 7.4 %partner_far.1 = (f32[1024,512]{1,0:T(8,128)}, bf16[1024,512]{1,0:T(8,128)(2,1)}) custom-call(s32[4]{0:T(128)} %pad_add_fusion.place_ref, bf16[512,512]{1,0:T(8,128)(2,1)} %collective-permute-done.9.refs_0_.refs_10_, bf16[512,512]{1,0:T(8,128)(2,1)} %collective-permute-done.10.refs_1_.refs_11_, bf16[512,512]{1,0:T(8,128)(2,1)} %collective-permute-done.13.refs_2_.refs_12_, ...), custom_call_target="tpu_custom_call" | custom-call | flops 524288 | bytes 524288 | tf_op jit(solution)/shard_map/partner_far/pallas_call | solution.py:230
  132.5 1.3 collective-permute-start.22
  133.9 0.8 copy-done.12
  134.9 5.7 %partner_last.1 = bf16[1024,512]{1,0:T(8,128)(2,1)} custom-call(s32[4]{0:T(128)} %pad_add_fusion.place_ref, bf16[512,512]{1,0:T(8,128)(2,1)} %collective-permute-done.17.refs_14_.refs_0_, bf16[512,512]{1,0:T(8,128)(2,1)} %collective-permute-done.18.refs_15_.refs_1_, bf16[512,512]{1,0:T(8,128)(2,1)} %copy-done.12, bf16[512,512]{1,0:T(8,128)(2,1)} %copy-done.13, ...), custom_call_target="tpu_custom_call" | custom-call | flops 524288 | bytes 524288 | tf_op jit(solution)/shard_map/partner_last/pallas_call | solution.py:230
  141.3 9.6 %own_columns.1 = bf16[1024,512]{1,0:T(8,128)(2,1)} custom-call(s32[4]{0:T(128)} %pad_add_fusion.place_ref, bf16[512,512]{1,0:T(8,128)(2,1)} %early_tokens.1.refs_0_, bf16[512,512]{1,0:T(8,128)(2,1)} %late_tokens.1.refs_1_, bf16[512,512]{1,0:T(8,128)(2,1)} %copy-done.2, bf16[512,512]{1,0:T(8,128)(2,1)} %copy-done.1, bf16[512,512]{1,0:T(8,128)(2,1)} %copy-done.4, ...), custom_call_target="tpu_custom_call" | custom-call | flops 524288 | bytes 524288 | tf_op jit(solution)/shard_map/own_columns/pallas_call | solution.py:230
  150.9 37.3 %collective-permute-done.22 = bf16[1024,512]{1,0:T(8,128)(2,1)S(1)} collective-permute-done((bf16[1024,512]{1,0:T(8,128)(2,1)}, bf16[1024,512]{1,0:T(8,128)(2,1)S(1)}, u32[]{:S(2)}, u32[]{:S(2)}) %collective-permute-start.22) | collective-permute-done | bytes 1048608 | tf_op jit(solution)/shard_map/ppermute | solution.py:34
  188.2 1.1 select_select_fusion
  (67 shorter events, 9.3 us)
Async XLA Ops:
  6.5 109.8 %all-gather.2.cloned.1.call-start = ((), (), s32[]{:S(2)}) async-start(), calls=%async_computation | async-start | bytes 8650752 | tf_op jit(solution)/shard_map/all_gather | solution.py:272
  9.8 37.6 %collective-permute-start = (bf16[160,512]{1,0:T(8,128)(2,1)}, bf16[160,512]{1,0:T(8,128)(2,1)S(1)}, u32[]{:S(2)}, u32[]{:S(2)}) collective-permute-start(bf16[160,512]{1,0:T(8,128)(2,1)} %tail_tokens.1), channel_id=1, source_target_pairs={{0,8},{8,16},{16,24},{24,32},{32,40},{40,48},{48,56},{56,64},{64,7... | collective-permute-start | bytes 491528 | tf_op jit(solution)/shard_map/ppermute | solution.py:264
  47.5 10.8 %collective-permute-start.2 = (bf16[512,512]{1,0:T(8,128)(2,1)}, bf16[512,512]{1,0:T(8,128)(2,1)S(1)}, u32[]{:S(2)}, u32[]{:S(2)}) collective-permute-start(bf16[512,512]{1,0:T(8,128)(2,1)} %late_tokens.1.refs_1_), channel_id=1, source_target_pairs={{1,0},{2,1},{3,2},{4,3},{5,4},{6,5},{7,6},{14,15},{13,14},{12,13},... | collective-permute-start | bytes 1572872 | tf_op jit(solution)/shard_map/ppermute | solution.py:26
  55.7 9.0 %collective-permute-start.1 = (bf16[512,512]{1,0:T(8,128)(2,1)}, bf16[512,512]{1,0:T(8,128)(2,1)S(1)}, u32[]{:S(2)}, u32[]{:S(2)}) collective-permute-start(bf16[512,512]{1,0:T(8,128)(2,1)} %early_tokens.1.refs_0_), channel_id=1, source_target_pairs={{1,0},{2,1},{3,2},{4,3},{5,4},{6,5},{7,6},{14,15},{13,14},{12,13},... | collective-permute-start | bytes 1572872 | tf_op jit(solution)/shard_map/ppermute | solution.py:26
  58.3 7.1 %collective-permute-start.4 = (bf16[512,512]{1,0:T(8,128)(2,1)S(1)}, bf16[512,512]{1,0:T(8,128)(2,1)S(1)}, u32[]{:S(2)}, u32[]{:S(2)}) collective-permute-start(bf16[512,512]{1,0:T(8,128)(2,1)S(1)} %collective-permute-done.2.refs_3_), channel_id=1, source_target_pairs={{1,0},{2,1},{3,2},{4,3},{5,4},{6,5},{14,15},{13,14},{12,13},{11,12... | collective-permute-start | bytes 1572872 | tf_op jit(solution)/shard_map/ppermute | solution.py:26
  64.7 1.4 collective-permute-start.3
  65.4 1.4 collective-permute-start.6
  66.1 1.4 collective-permute-start.5
  66.9 2.8 %collective-permute-start.8 = (bf16[512,512]{1,0:T(8,128)(2,1)S(1)}, bf16[512,512]{1,0:T(8,128)(2,1)S(1)}, u32[]{:S(2)}, u32[]{:S(2)}) collective-permute-start(bf16[512,512]{1,0:T(8,128)(2,1)S(1)} %collective-permute-done.6.refs_7_), channel_id=1, source_target_pairs={{1,0},{2,1},{3,2},{4,3},{14,15},{13,14},{12,13},{11,12},{17,16},{1... | collective-permute-start | bytes 1572872 | tf_op jit(solution)/shard_map/ppermute | solution.py:26
  67.6 3.6 %collective-permute-start.7 = (bf16[512,512]{1,0:T(8,128)(2,1)S(1)}, bf16[512,512]{1,0:T(8,128)(2,1)S(1)}, u32[]{:S(2)}, u32[]{:S(2)}) collective-permute-start(bf16[512,512]{1,0:T(8,128)(2,1)S(1)} %collective-permute-done.5.refs_6_), channel_id=1, source_target_pairs={{1,0},{2,1},{3,2},{4,3},{14,15},{13,14},{12,13},{11,12},{17,16},{1... | collective-permute-start | bytes 1572872 | tf_op jit(solution)/shard_map/ppermute | solution.py:26
  68.3 4.4 %collective-permute-start.14 = (bf16[512,512]{1,0:T(8,128)(2,1)S(1)}, bf16[512,512]{1,0:T(8,128)(2,1)S(1)}, u32[]{:S(2)}, u32[]{:S(2)}) collective-permute-start(bf16[512,512]{1,0:T(8,128)(2,1)S(1)} %copy-done), channel_id=1, source_target_pairs={{0,1},{1,2},{2,3},{15,14},{14,13},{13,12},{16,17},{17,18},{18,19},... | collective-permute-start | bytes 1572872 | tf_op jit(solution)/shard_map/ppermute | solution.py:30
  69.0 4.4 %collective-permute-start.11 = (bf16[512,512]{1,0:T(8,128)(2,1)}, bf16[512,512]{1,0:T(8,128)(2,1)S(1)}, u32[]{:S(2)}, u32[]{:S(2)}) collective-permute-start(bf16[512,512]{1,0:T(8,128)(2,1)} %early_tokens.1.refs_0_), channel_id=1, source_target_pairs={{0,1},{1,2},{2,3},{15,14},{14,13},{13,12},{16,17},{17,18},{18,19},... | collective-permute-start | bytes 1572872 | tf_op jit(solution)/shard_map/ppermute | solution.py:30
  69.7 5.1 %collective-permute-start.10 = (bf16[512,512]{1,0:T(8,128)(2,1)S(1)}, bf16[512,512]{1,0:T(8,128)(2,1)}, u32[]{:S(2)}, u32[]{:S(2)}) collective-permute-start(bf16[512,512]{1,0:T(8,128)(2,1)S(1)} %collective-permute-done.8.refs_9_), channel_id=1, source_target_pairs={{1,0},{2,1},{3,2},{14,15},{13,14},{12,13},{17,16},{18,17},{19,18},... | collective-permute-start | bytes 1572872 | tf_op jit(solution)/shard_map/ppermute | solution.py:26
  71.2 5.1 %collective-permute-start.9 = (bf16[512,512]{1,0:T(8,128)(2,1)S(1)}, bf16[512,512]{1,0:T(8,128)(2,1)}, u32[]{:S(2)}, u32[]{:S(2)}) collective-permute-start(bf16[512,512]{1,0:T(8,128)(2,1)S(1)} %collective-permute-done.7.refs_8_), channel_id=1, source_target_pairs={{1,0},{2,1},{3,2},{14,15},{13,14},{12,13},{17,16},{18,17},{19,18},... | collective-permute-start | bytes 1572872 | tf_op jit(solution)/shard_map/ppermute | solution.py:26
  72.7 5.1 %collective-permute-start.15 = (bf16[512,512]{1,0:T(8,128)(2,1)S(1)}, bf16[512,512]{1,0:T(8,128)(2,1)S(1)}, u32[]{:S(2)}, u32[]{:S(2)}) collective-permute-start(bf16[512,512]{1,0:T(8,128)(2,1)S(1)} %collective-permute-done.14.refs_7_.refs_21_), channel_id=1, source_target_pairs={{1,2},{2,3},{14,13},{13,12},{17,18},{18,19},{30,29},{29,28},{33,34... | collective-permute-start | bytes 1572872 | tf_op jit(solution)/shard_map/ppermute | solution.py:30
  73.4 5.9 %collective-permute-start.12 = (bf16[512,512]{1,0:T(8,128)(2,1)S(1)}, bf16[512,512]{1,0:T(8,128)(2,1)}, u32[]{:S(2)}, u32[]{:S(2)}) collective-permute-start(bf16[512,512]{1,0:T(8,128)(2,1)S(1)} %collective-permute-done.11.refs_6_.refs_20_), channel_id=1, source_target_pairs={{1,2},{2,3},{14,13},{13,12},{17,18},{18,19},{30,29},{29,28},{33,34... | collective-permute-start | bytes 1572872 | tf_op jit(solution)/shard_map/ppermute | solution.py:30
  74.9 48.8 %collective-permute-start.18 = (bf16[512,512]{1,0:T(8,128)(2,1)}, bf16[512,512]{1,0:T(8,128)(2,1)}, u32[]{:S(2)}, u32[]{:S(2)}) collective-permute-start(bf16[512,512]{1,0:T(8,128)(2,1)} %collective-permute-done.10.refs_1_.refs_11_), channel_id=1, source_target_pairs={{1,0},{2,1},{14,15},{13,14},{17,16},{18,17},{30,31},{29,30},{33,32... | collective-permute-start | bytes 1572872 | tf_op jit(solution)/shard_map/ppermute | solution.py:26
  76.3 47.4 %collective-permute-start.17 = (bf16[512,512]{1,0:T(8,128)(2,1)}, bf16[512,512]{1,0:T(8,128)(2,1)}, u32[]{:S(2)}, u32[]{:S(2)}) collective-permute-start(bf16[512,512]{1,0:T(8,128)(2,1)} %collective-permute-done.9.refs_0_.refs_10_), channel_id=1, source_target_pairs={{1,0},{2,1},{14,15},{13,14},{17,16},{18,17},{30,31},{29,30},{33,32... | collective-permute-start | bytes 1572872 | tf_op jit(solution)/shard_map/ppermute | solution.py:26
  77.8 47.3 %collective-permute-start.16 = (bf16[512,512]{1,0:T(8,128)(2,1)S(1)}, bf16[512,512]{1,0:T(8,128)(2,1)}, u32[]{:S(2)}, u32[]{:S(2)}) collective-permute-start(bf16[512,512]{1,0:T(8,128)(2,1)S(1)} %collective-permute-done.15.refs_5_.refs_17_), channel_id=1, source_target_pairs={{2,3},{13,12},{18,19},{29,28},{34,35},{45,44},{50,51},{61,60},{66,... | collective-permute-start | bytes 1572872 | tf_op jit(solution)/shard_map/ppermute | solution.py:30
  79.3 45.8 %collective-permute-start.13 = (bf16[512,512]{1,0:T(8,128)(2,1)}, bf16[512,512]{1,0:T(8,128)(2,1)}, u32[]{:S(2)}, u32[]{:S(2)}) collective-permute-start(bf16[512,512]{1,0:T(8,128)(2,1)} %collective-permute-done.12.refs_4_.refs_16_), channel_id=1, source_target_pairs={{2,3},{13,12},{18,19},{29,28},{34,35},{45,44},{50,51},{61,60},{66,... | collective-permute-start | bytes 1572872 | tf_op jit(solution)/shard_map/ppermute | solution.py:30
  123.7 10.2 %collective-permute-start.19 = (bf16[512,512]{1,0:T(8,128)(2,1)}, bf16[512,512]{1,0:T(8,128)(2,1)S(1)}, u32[]{:S(2)}, u32[]{:S(2)}) collective-permute-start(bf16[512,512]{1,0:T(8,128)(2,1)} %collective-permute-done.17.refs_14_.refs_0_), channel_id=1, source_target_pairs={{1,0},{14,15},{17,16},{30,31},{33,32},{46,47},{49,48},{62,63},{65,... | collective-permute-start | bytes 1572872 | tf_op jit(solution)/shard_map/ppermute | solution.py:26
  124.4 9.5 %collective-permute-start.20 = (bf16[512,512]{1,0:T(8,128)(2,1)}, bf16[512,512]{1,0:T(8,128)(2,1)S(1)}, u32[]{:S(2)}, u32[]{:S(2)}) collective-permute-start(bf16[512,512]{1,0:T(8,128)(2,1)} %collective-permute-done.18.refs_15_.refs_1_), channel_id=1, source_target_pairs={{1,0},{14,15},{17,16},{30,31},{33,32},{46,47},{49,48},{62,63},{65,... | collective-permute-start | bytes 1572872 | tf_op jit(solution)/shard_map/ppermute | solution.py:26
  132.5 55.7 %collective-permute-start.22 = (bf16[1024,512]{1,0:T(8,128)(2,1)}, bf16[1024,512]{1,0:T(8,128)(2,1)S(1)}, u32[]{:S(2)}, u32[]{:S(2)}) collective-permute-start(bf16[1024,512]{1,0:T(8,128)(2,1)} %get-tuple-element.38), channel_id=1, source_target_pairs={{2,6},{3,7},{13,9},{12,8},{18,22},{19,23},{29,25},{28,24},{34,38},... | collective-permute-start | bytes 3145736 | tf_op jit(solution)/shard_map/ppermute | solution.py:34
  140.5 47.7 %collective-permute-start.21 = (bf16[1024,512]{1,0:T(8,128)(2,1)}, bf16[1024,512]{1,0:T(8,128)(2,1)S(1)}, u32[]{:S(2)}, u32[]{:S(2)}) collective-permute-start(bf16[1024,512]{1,0:T(8,128)(2,1)} %partner_last.1), channel_id=1, source_target_pairs={{0,4},{1,5},{15,11},{14,10},{16,20},{17,21},{31,27},{30,26},{32,36... | collective-permute-start | bytes 3145736 | tf_op jit(solution)/shard_map/ppermute | solution.py:34
  (16 other events, 393.1 us)
Sparse Core Ops, SparseCore 0:
  47.6 68.7 all-gather.1

commit v3 on v2

v3 whole, which is shorter than its diff:
```python
import functools

import jax
import jax.numpy as jnp
from jax import lax
from jax.experimental import pallas as pl
from jax.experimental.pallas import tpu as pltpu
from jax.sharding import Mesh, PartitionSpec as P

SEQ = ("zh", "y", "x", "c")
PLANE = ("y", "x", "c")
TP = ("th", "tl")
LINE = ("c",) + TP
LANES = 128
LINE_LEN = 8
WORKERS = 4
VMEM = 60 << 20


def on_line(pairs):
    place = lambda u, core: core * LINE_LEN + (u if core == 0 else LINE_LEN - 1 - u)
    return [(place(a, core), place(b, core)) for core in (0, 1) for a, b in pairs]


def inward(block, step):
    return lax.ppermute(block, LINE, on_line([(u, u - 1) for u in range(1, LINE_LEN + 1 - step)]))


def outward(block, step):
    return lax.ppermute(block, LINE, on_line([(u, u + 1) for u in range(step - 1, WORKERS - 1)]))


def deliver(block, workers):
    return lax.ppermute(block, LINE, on_line([(u, u + WORKERS) for u in workers]))


def feature(rows, taps):
    return (
        taps[0:1] * rows
        + taps[1:2] * pltpu.roll(rows, 1, 0)
        + taps[2:3] * pltpu.roll(rows, 2, 0)
    )


def toeplitz(filt, toep):
    groups, taps = filt.shape
    lag = lax.broadcasted_iota(jnp.int32, (taps, 2 * taps), 0)
    col = lax.broadcasted_iota(jnp.int32, (taps, 2 * taps), 1)
    flip = jnp.where(lag + col == taps, 1.0, 0.0).astype(jnp.bfloat16)
    first = jnp.dot(filt, flip, preferred_element_type=jnp.float32)
    for g in range(groups):
        wide = jnp.broadcast_to(first[g : g + 1], (taps, 2 * taps))
        wide = pltpu.roll(wide, 0, 1, stride=1, stride_axis=0)
        toep[g * taps : (g + 1) * taps] = wide.astype(jnp.bfloat16)


def convolve(gated, query, groups, taps, toep):
    group_of = lax.broadcasted_iota(jnp.int32, (taps, 2 * LANES), 1) % LANES // (LANES // groups)
    pieces = []
    for pair in range(query.shape[0] // taps // 2):
        base = 2 * pair * taps
        window = jnp.concatenate(
            [gated[base : base + 2 * taps], gated[base + taps : base + 3 * taps]], axis=1
        )
        every = jnp.dot(toep[...], window, preferred_element_type=jnp.float32)
        conv = every[:taps]
        for g in range(1, groups):
            conv = jnp.where(group_of == g, every[g * taps : (g + 1) * taps], conv)
        for k in range(2):
            at = base + k * taps
            piece = conv[:, k * LANES : (k + 1) * LANES] * query[at : at + taps]
            pieces.append(piece.astype(jnp.bfloat16))
    return pieces


def local_kernel(late, x_ref, taps_ref, filt_ref, halo_ref, *refs):
    out_ref, tail_ref = refs[0], refs[1] if late else None
    rows_ref, taps_held, filt_held, halo_held, toep, sems = refs[-6:]
    streams, count = rows_ref.shape[:2]
    tiles, groups, taps = filt_held.shape
    first = x_ref.shape[1] - count if late else 0
    copies = [pltpu.make_async_copy(filt_ref, filt_held, sems.at[0])]
    copies.append(pltpu.make_async_copy(taps_ref, taps_held, sems.at[1]))
    for s in range(streams):
        source = x_ref.at[s, pl.ds(first, count)]
        copies.append(pltpu.make_async_copy(source, rows_ref.at[s], sems.at[2 + s]))
    if not late:
        copies.append(pltpu.make_async_copy(halo_ref, halo_held, sems.at[2 + streams]))
    for copy in copies:
        copy.start()
    copies[0].wait()

    @pl.loop(0, tiles)
    def _(tile):
        toeplitz(filt_held[tile], toep.at[tile])

    for copy in copies[1:]:
        copy.wait()

    @pl.loop(0, tiles)
    def _(tile):
        lanes = pl.ds(pl.multiple_of(tile * LANES, LANES), LANES)
        if late:
            rows = [rows_ref[s, :, lanes].astype(jnp.float32) for s in range(streams)]
            featured = [feature(rows[s], taps_held[s, :, lanes]) for s in range(streams)]
            gated = (featured[1] * featured[2])[16:].astype(jnp.bfloat16)
            query = featured[0][taps + 16 :]
            raw = [r[count - 8 :] for r in rows]
            raw.append(jnp.zeros_like(raw[0]))
            tail_ref[:taps, lanes] = gated[gated.shape[0] - taps :]
            tail_ref[taps:, lanes] = jnp.concatenate(raw, axis=0).astype(jnp.bfloat16)
        else:
            before = halo_held[taps:, lanes].astype(jnp.float32)
            featured = []
            for s in range(streams):
                rows = rows_ref[s, :, lanes].astype(jnp.float32)
                rows = jnp.concatenate([before[8 * s : 8 * s + 8], rows], axis=0)
                featured.append(feature(rows, taps_held[s, :, lanes])[8:])
            gated = (featured[1] * featured[2]).astype(jnp.bfloat16)
            gated = jnp.concatenate([halo_held[:taps, lanes], gated], axis=0)
            query = featured[0]
        for k, piece in enumerate(convolve(gated, query, groups, taps, toep.at[tile])):
            out_ref[k * taps : (k + 1) * taps, lanes] = piece


def local_part(x, halo, short_taps, long_filter):
    streams, tokens, channels = x.shape
    groups, taps = long_filter.shape
    filt = long_filter.reshape(channels // LANES, -1, taps)
    half, tail = tokens // 2, taps + 32
    late = halo is None
    shapes = [(half, channels), (tail, channels)] if late else [(half, channels)]
    return pl.pallas_call(
        functools.partial(local_kernel, late),
        in_specs=[pl.BlockSpec(memory_space=pl.ANY)] * 4,
        out_specs=[pl.BlockSpec(memory_space=pltpu.VMEM)] * len(shapes),
        out_shape=[jax.ShapeDtypeStruct(shape, jnp.bfloat16) for shape in shapes],
        scratch_shapes=[
            pltpu.VMEM((streams, half + taps + 16 if late else half, channels), jnp.bfloat16),
            pltpu.VMEM(short_taps.shape, jnp.float32),
            pltpu.VMEM(filt.shape, jnp.bfloat16),
            pltpu.VMEM((tail, channels), jnp.bfloat16),
            pltpu.VMEM((channels // LANES, groups * LANES // channels * taps, 2 * taps), jnp.bfloat16),
            pltpu.SemaphoreType.DMA((streams + 3,)),
        ],
        compiler_params=pltpu.CompilerParams(vmem_limit_bytes=VMEM),
        cost_estimate=pl.CostEstimate(flops=1 << 30, bytes_accessed=4 << 20, transcendentals=0),
        name="late_tokens" if late else "early_tokens",
    )(x, short_taps, filt, filt if late else halo)


def project_kernel(slots, side, outs, has_start, place_ref, *refs):
    total = sum(count for _, options in slots for _, count in options)
    x_refs, w_ref = refs[:total], refs[total]
    held, weight, acc, start, x_sems, w_sems, start_sem = refs[-7:]
    out_refs = refs[len(refs) - 7 - outs : len(refs) - 7]
    at, toward, th, u = [place_ref[i] for i in range(4)]
    parts, half, depth = held.shape[1:]
    per_zh = w_ref.shape[0]

    def fetch(slot, first, count, part):
        source = x_refs[first + part] if count > 1 else x_refs[first].at[pl.ds(part * half, half)]
        return pltpu.make_async_copy(source, held.at[slot, part], x_sems.at[slot, part])

    def rows(slot, y, z):
        return pltpu.make_async_copy(w_ref.at[y, :, z], weight.at[slot], w_sems.at[slot])

    @pl.when(u < WORKERS)
    def _():
        firsts = []
        position = 0
        for slot, (limit, options) in enumerate(slots):
            distance = options[0][0]
            if limit is not None:
                distance = jnp.where(u < limit, distance, options[1][0])
            block = jnp.clip(at + toward * distance, 0, LINE_LEN - 1)
            upper = jnp.where(block >= per_zh, 1, 0)
            column = th if side == 0 else 1 - th
            rows(slot, block - per_zh * upper, 2 * upper + column).start()
            firsts.append((position, options[0][1]))
            for option, (_, count) in enumerate(options):
                for part in range(parts):
                    copy = fetch(slot, position, count, part)
                    if limit is None:
                        copy.start()
                    else:
                        pl.when(u < limit if option == 0 else u >= limit)(copy.start)
                position += count
        if has_start:
            from_start = pltpu.make_async_copy(refs[total + 1], start, start_sem)
            from_start.start()

        for slot in range(len(slots)):
            rows(slot, 0, 0).wait()
            for part in range(parts):
                fetch(slot, *firsts[slot], part).wait()
            term = jnp.dot(
                held[slot].reshape(parts * half, depth),
                weight[slot].reshape(depth, weight.shape[-1]),
                preferred_element_type=jnp.float32,
            )
            if slot > 0:
                term = acc[...] + term
            if slot < len(slots) - 1:
                acc[...] = term
            else:
                if has_start:
                    from_start.wait()
                    term = start[...] + term
                for out_ref in out_refs:
                    out_ref[...] = term.astype(out_ref.dtype)


def project(slots, place, weights, side, start, kinds, name):
    half, depth = slots[0][1][0][1][0].shape
    ys, members, zs, rows, columns = weights.shape
    blocks, tokens = len(slots), 2 * half
    operands = [part for _, options in slots for _, block in options for part in block] + [weights]
    if start is not None:
        operands.append(start)
    shape_of_slots = tuple(
        (limit, tuple((distance, len(block)) for distance, block in options)) for limit, options in slots
    )
    return pl.pallas_call(
        functools.partial(project_kernel, shape_of_slots, side, len(kinds), start is not None),
        grid_spec=pltpu.PrefetchScalarGridSpec(
            num_scalar_prefetch=1,
            grid=(1,),
            in_specs=[pl.BlockSpec(memory_space=pl.ANY)] * len(operands),
            out_specs=[pl.BlockSpec((tokens, columns), lambda i, place: (0, 0))] * len(kinds),
            scratch_shapes=[
                pltpu.VMEM((blocks, 2, half, depth), jnp.bfloat16),
                pltpu.VMEM((blocks, members, rows, columns), jnp.bfloat16),
                pltpu.VMEM((tokens, columns), jnp.float32),
                pltpu.VMEM((tokens, columns) if start is not None else (8, LANES), jnp.float32),
                pltpu.SemaphoreType.DMA((blocks, 2)),
                pltpu.SemaphoreType.DMA((blocks,)),
                pltpu.SemaphoreType.DMA,
            ],
        ),
        out_shape=[jax.ShapeDtypeStruct((tokens, columns), kind) for kind in kinds],
        compiler_params=pltpu.CompilerParams(vmem_limit_bytes=VMEM),
        cost_estimate=pl.CostEstimate(
            flops=tokens * columns, bytes_accessed=tokens * columns, transcendentals=0
        ),
        name=name,
    )(place, *operands)


def per_device(projected, short_taps, long_filter, out_weight):
    core, at, th = lax.axis_index("c"), lax.axis_index(TP), lax.axis_index("th")
    u = jnp.where(core == 0, at, LINE_LEN - 1 - at)
    toward = jnp.where(core == 0, 1, -1)
    place = jnp.stack([at, toward, th, u]).astype(jnp.int32)
    in_order = lax.optimization_barrier

    late, tail = local_part(projected, None, short_taps, long_filter)
    next_seq = [(i, i + 1) for i in range(lax.axis_size(SEQ) - 1)]
    halo = lax.ppermute(tail, SEQ, next_seq)

    own_shard, place, _ = in_order((out_weight, place, late))
    shard = lax.all_gather(own_shard, ("zh", "th"), axis=0, tiled=True)
    projected, halo, shard = in_order((projected, halo, shard))
    weights = lax.all_gather(shard, PLANE, axis=0, tiled=True)
    projected, halo, _ = in_order((projected, halo, shard))
    (early,) = local_part(projected, halo, short_taps, long_filter)
    rows, columns = out_weight.shape
    parts = lax.axis_size(("zh", "th"))
    weights = weights.reshape(lax.axis_size("y"), -1, parts, rows, columns)

    came = [(early, late)]
    back = [(early, late)]
    for step in range(1, LINE_LEN - 2):
        before, behind = came[-1]
        before = inward(before, step)
        behind = inward(behind, step)
        came.append((before, behind))
        if step > 2:
            back.append(tuple(outward(part, step - 2) for part in back[-1]))

    kinds = (jnp.float32, jnp.bfloat16)
    near = [(None, [(d, came[d])]) for d in range(5)]
    (total,) = project(near, place, weights, 1, None, kinds[:1], "partner_near")
    fifth = came[5]
    came.append(tuple(inward(part, LINE_LEN - 2) for part in fifth))
    sixth, total, back[3] = in_order((came[6], total, back[3]))
    came.append(tuple(inward(part, LINE_LEN - 1) for part in sixth))
    far = [
        (3, [(5, fifth), (-3, back[3])]),
        (2, [(6, sixth), (-2, back[2])]),
        (None, [(-1, back[1])]),
    ]
    total, ready = project(far, place, weights, 1, total, kinds, "partner_far")
    sent_first = deliver(ready, (1, 2, 3))
    last, total = in_order((came[7], total))
    (ready,) = project([(None, [(7, last)])], place, weights, 1, total, kinds[1:], "partner_last")
    sent_last = deliver(ready, (0,))

    every = near + far[:2] + [(1, [(7, last), (-1, back[1])])]
    (mine,) = project(every, place, weights, 0, None, kinds[1:], "own_columns")
    given = jnp.where(u == WORKERS, sent_last, sent_first)
    return jnp.where(u < WORKERS, mine, given)


def solution(mesh):
    split = Mesh(mesh.devices.reshape(2, 4, 4, 2, 2, WORKERS), SEQ + TP)
    in_specs = (P(None, SEQ, TP), P(None, None, TP), P(TP, None), P(SEQ, TP))
    return jax.shard_map(
        per_device, mesh=split, in_specs=in_specs, out_specs=P(SEQ, TP), check_vma=False
    )
```

time: 200 us -> 194 us (0.970); the launches traced: 196 us -> 193 us
  Pallas kernels: 44.2 us -> 19.2 us
  waiting for transfers between devices: 78.6 us -> 100 us
    pallas_call x4, Pallas kernels: 30 us -> 8.13 us  [project(): pl.pallas_call(functools.partial(project_kernel, shape_of_slots, side, le...]
    ppermute x2, waiting for transfers between devices: 37.3 us -> 54.8 us  [deliver(): lax.ppermute(block, LINE, on_line([(u, u + WORKERS) for u in workers]))]
    all_gather x1, waiting for transfers between devices: 35.6 us -> 39.7 us  [per_device(): weights = lax.all_gather(shard, PLANE, axis=0, tiled=True)]
    pallas_call x3 -> x2, Pallas kernels: 14.3 us -> 11.1 us  [local_part(): pl.pallas_call(functools.partial(local_kernel, late), in_specs=[pl.BlockS...]
  transfers between devices with their start and end apart: 24 -> 24, of which waited for: 3 -> 3; matrix products, arithmetic and copies ran while one was open for 0% -> 0% of each run, Pallas kernels for 21% -> 7%
where the time goes in v3:
time: 194 us; the launch traced here: 193 us
  waiting for transfers between devices  100 us (52%)
  starting transfers between devices  29.8 us (15%)
  blocking collectives  26.9 us (14%)
  Pallas kernels  19.2 us (10%)
  between operations  13.8 us (7%)
    ppermute x2, waiting for transfers between devices, deliver(): lax.ppermute(block, LINE, on_line([(u, u + WORKERS) for u in workers]))  54.8 us
    all_gather x1, waiting for transfers between devices, per_device(): weights = lax.all_gather(shard, PLANE, axis=0, tiled=True)  39.7 us
    all_gather x1, blocking collectives, per_device(): shard = lax.all_gather(own_shard, ('zh', 'th'), axis=0, tiled=True)  26.9 us
    ppermute x14, starting transfers between devices, inward(): lax.ppermute(block, LINE, on_line([(u, u - 1) for u in range(1, LINE_LEN...  16.7 us
    pallas_call x2, Pallas kernels, local_part(): pl.pallas_call(functools.partial(local_kernel, late), in_specs=[pl.BlockS...  11.1 us
    pallas_call x4, Pallas kernels, project(): pl.pallas_call(functools.partial(project_kernel, shape_of_slots, side, le...  8.13 us
    ppermute x6, starting transfers between devices, outward(): lax.ppermute(block, LINE, on_line([(u, u + 1) for u in range(step - 1, WO...  6.47 us
    ppermute x14, waiting for transfers between devices, inward(): lax.ppermute(block, LINE, on_line([(u, u - 1) for u in range(1, LINE_LEN...  5.7 us
  transfers between devices with their start and end apart: 24, of which 3 were waited for; matrix products, arithmetic and copies ran while one was open for 0% of the time, Pallas kernels for 7%

profile of v3, /device:TPU:1, one launch (start us, length us, event | category | flops | bytes accessed | tf_op | source)
XLA Modules:
  0.0 192.7 jit_solution(1288063719995350597)
XLA Ops:
  6.5 5.7 %late_tokens.1 = (bf16[512,512]{1,0:T(8,128)(2,1)}, bf16[160,512]{1,0:T(8,128)(2,1)}) custom-call(bf16[3,1024,512]{2,1,0:T(8,128)(2,1)} %x_ref.2, f32[3,3,512]{2,1,0:T(4,128)} %taps_ref.3, bf16[4,8,128]{2,1,0:T(8,128)(2,1)} %bitcast.10, bf16[4,8,128]{2,1,0:T(8,128)(2,1)} %bitcast.11), custom_call_target="tpu_custom_call" | custom-call | flops 1073741824 | bytes 4194304 | tf_op jit(solution)/shard_map/late_tokens/pallas_call | solution.py:133
  12.3 4.6 %collective-permute-start = (bf16[160,512]{1,0:T(8,128)(2,1)}, bf16[160,512]{1,0:T(8,128)(2,1)S(1)}, u32[]{:S(2)}, u32[]{:S(2)}) collective-permute-start(bf16[160,512]{1,0:T(8,128)(2,1)} %get-tuple-element.28), channel_id=1, source_target_pairs={{0,8},{8,16},{16,24},{24,32},{32,40},{40,48},{48,56},{56,64},{64,7... | collective-permute-start | bytes 491528 | tf_op jit(solution)/shard_map/ppermute | solution.py:259
  17.6 26.9 %all_gather.6 = bf16[256,512]{1,0:T(8,128)(2,1)} all-gather(bf16[64,512]{1,0:T(8,128)(2,1)S(1)} %copy-done.14), channel_id=1, replica_groups=mesh['zh'=2,'y'=4,'x'=4,'c'=2,'th'=2,'tl'=4] {'zh','th'}, dimensions={0}, use_global_device_ids=true | all-gather | bytes 327680 | tf_op jit(solution)/shard_map/all_gather | solution.py:262
  44.5 2.6 %collective-permute-start.2 = (bf16[512,512]{1,0:T(8,128)(2,1)}, bf16[512,512]{1,0:T(8,128)(2,1)S(1)}, u32[]{:S(2)}, u32[]{:S(2)}) collective-permute-start(bf16[512,512]{1,0:T(8,128)(2,1)} %get-tuple-element.26.refs_1_), channel_id=1, source_target_pairs={{1,0},{2,1},{3,2},{4,3},{5,4},{6,5},{7,6},{14,15},{13,14},{12,13},... | collective-permute-start | bytes 1572872 | tf_op jit(solution)/shard_map/ppermute | solution.py:26
  47.1 5.4 %early_tokens.1.refs_0_ = bf16[512,512]{1,0:T(8,128)(2,1)} custom-call(bf16[3,1024,512]{2,1,0:T(8,128)(2,1)} %x_ref.2, f32[3,3,512]{2,1,0:T(4,128)} %taps_ref.3, bf16[4,8,128]{2,1,0:T(8,128)(2,1)} %bitcast.12, bf16[160,512]{1,0:T(8,128)(2,1)} %copy-done.15), custom_call_target="tpu_custom_call" | custom-call | flops 1073741824 | bytes 4194304 | tf_op jit(solution)/shard_map/early_tokens/pallas_call | solution.py:133
  52.5 2.6 %collective-permute-start.1 = (bf16[512,512]{1,0:T(8,128)(2,1)}, bf16[512,512]{1,0:T(8,128)(2,1)S(1)}, u32[]{:S(2)}, u32[]{:S(2)}) collective-permute-start(bf16[512,512]{1,0:T(8,128)(2,1)} %early_tokens.1.refs_0_), channel_id=1, source_target_pairs={{1,0},{2,1},{3,2},{4,3},{5,4},{6,5},{7,6},{14,15},{13,14},{12,13},... | collective-permute-start | bytes 1572872 | tf_op jit(solution)/shard_map/ppermute | solution.py:26
  55.9 5.7 %collective-permute-done.1.refs_2_ = bf16[512,512]{1,0:T(8,128)(2,1)S(1)} collective-permute-done((bf16[512,512]{1,0:T(8,128)(2,1)}, bf16[512,512]{1,0:T(8,128)(2,1)S(1)}, u32[]{:S(2)}, u32[]{:S(2)}) %collective-permute-start.1) | collective-permute-done | bytes 524320 | tf_op jit(solution)/shard_map/ppermute | solution.py:26
  67.3 1.5 collective-permute-start.14
  68.8 1.5 collective-permute-start.10
  70.3 1.5 collective-permute-start.9
  71.8 1.5 collective-permute-start.18
  73.2 1.5 collective-permute-start.15
  74.7 1.4 collective-permute-start.12
  76.1 1.5 collective-permute-start.11
  77.6 39.7 %all-gather.2.cloned.1.call-done = bf16[8192,512]{1,0:T(8,128)(2,1)} async-done(((bf16[256,512]{1,0:T(8,128)(2,1)}), bf16[8192,512]{1,0:T(8,128)(2,1)}) %all-gather.2.cloned.1.call-update) | async-done | bytes 8388624 | tf_op jit(solution)/shard_map/all_gather | solution.py:264
  117.3 2.2 %partner_near.1.refs_11_ = f32[1024,512]{1,0:T(8,128)} custom-call(s32[4]{0:T(128)} %pad_add_fusion.place_ref, bf16[512,512]{1,0:T(8,128)(2,1)} %early_tokens.1.refs_0_, bf16[512,512]{1,0:T(8,128)(2,1)} %get-tuple-element.26.refs_1_, bf16[512,512]{1,0:T(8,128)(2,1)} %copy-done.2, bf16[512,512]{1,0:T(8,128)(2,1)} %copy-done.1, bf16[512,512]{1,0:T(8,128)(2,1)} %copy-done.4, ...), custom_call_target="tpu_custom_call" | custom-call | flops 524288 | bytes 524288 | tf_op jit(solution)/shard_map/partner_near/pallas_call | solution.py:224
  121.0 2.4 %partner_far.1 = (f32[1024,512]{1,0:T(8,128)}, bf16[1024,512]{1,0:T(8,128)(2,1)}) custom-call(s32[4]{0:T(128)} %pad_add_fusion.place_ref, bf16[512,512]{1,0:T(8,128)(2,1)} %collective-permute-done.9.refs_0_.refs_10_, bf16[512,512]{1,0:T(8,128)(2,1)} %collective-permute-done.10.refs_1_.refs_11_, bf16[512,512]{1,0:T(8,128)(2,1)} %collective-permute-done.15.refs_2_.refs_12_, ...), custom_call_target="tpu_custom_call" | custom-call | flops 524288 | bytes 524288 | tf_op jit(solution)/shard_map/partner_far/pallas_call | solution.py:224
  123.4 1.3 collective-permute-start.22
  124.7 0.8 copy-done.12
  125.7 1.7 partner_last.1
  127.4 0.7 collective-permute-start.21
  128.1 1.9 own_columns.1
  130.0 54.8 %collective-permute-done.22 = bf16[1024,512]{1,0:T(8,128)(2,1)S(1)} collective-permute-done((bf16[1024,512]{1,0:T(8,128)(2,1)}, bf16[1024,512]{1,0:T(8,128)(2,1)S(1)}, u32[]{:S(2)}, u32[]{:S(2)}) %collective-permute-start.22) | collective-permute-done | bytes 1048608 | tf_op jit(solution)/shard_map/ppermute | solution.py:34
  184.8 1.1 select_select_fusion
  (66 shorter events, 8.6 us)
Async XLA Ops:
  6.5 110.7 %all-gather.2.cloned.1.call-start = ((), (), s32[]{:S(2)}) async-start(), calls=%async_computation | async-start | bytes 8650752 | tf_op jit(solution)/shard_map/all_gather | solution.py:264
  12.3 32.2 %collective-permute-start = (bf16[160,512]{1,0:T(8,128)(2,1)}, bf16[160,512]{1,0:T(8,128)(2,1)S(1)}, u32[]{:S(2)}, u32[]{:S(2)}) collective-permute-start(bf16[160,512]{1,0:T(8,128)(2,1)} %get-tuple-element.28), channel_id=1, source_target_pairs={{0,8},{8,16},{16,24},{24,32},{32,40},{40,48},{48,56},{56,64},{64,7... | collective-permute-start | bytes 491528 | tf_op jit(solution)/shard_map/ppermute | solution.py:259
  44.5 10.7 %collective-permute-start.2 = (bf16[512,512]{1,0:T(8,128)(2,1)}, bf16[512,512]{1,0:T(8,128)(2,1)S(1)}, u32[]{:S(2)}, u32[]{:S(2)}) collective-permute-start(bf16[512,512]{1,0:T(8,128)(2,1)} %get-tuple-element.26.refs_1_), channel_id=1, source_target_pairs={{1,0},{2,1},{3,2},{4,3},{5,4},{6,5},{7,6},{14,15},{13,14},{12,13},... | collective-permute-start | bytes 1572872 | tf_op jit(solution)/shard_map/ppermute | solution.py:26
  52.5 9.0 %collective-permute-start.1 = (bf16[512,512]{1,0:T(8,128)(2,1)}, bf16[512,512]{1,0:T(8,128)(2,1)S(1)}, u32[]{:S(2)}, u32[]{:S(2)}) collective-permute-start(bf16[512,512]{1,0:T(8,128)(2,1)} %early_tokens.1.refs_0_), channel_id=1, source_target_pairs={{1,0},{2,1},{3,2},{4,3},{5,4},{6,5},{7,6},{14,15},{13,14},{12,13},... | collective-permute-start | bytes 1572872 | tf_op jit(solution)/shard_map/ppermute | solution.py:26
  55.2 7.1 %collective-permute-start.4 = (bf16[512,512]{1,0:T(8,128)(2,1)S(1)}, bf16[512,512]{1,0:T(8,128)(2,1)S(1)}, u32[]{:S(2)}, u32[]{:S(2)}) collective-permute-start(bf16[512,512]{1,0:T(8,128)(2,1)S(1)} %collective-permute-done.2.refs_3_), channel_id=1, source_target_pairs={{1,0},{2,1},{3,2},{4,3},{5,4},{6,5},{14,15},{13,14},{12,13},{11,12... | collective-permute-start | bytes 1572872 | tf_op jit(solution)/shard_map/ppermute | solution.py:26
  61.6 1.4 collective-permute-start.3
  62.3 2.8 %collective-permute-start.6 = (bf16[512,512]{1,0:T(8,128)(2,1)S(1)}, bf16[512,512]{1,0:T(8,128)(2,1)S(1)}, u32[]{:S(2)}, u32[]{:S(2)}) collective-permute-start(bf16[512,512]{1,0:T(8,128)(2,1)S(1)} %collective-permute-done.4.refs_5_), channel_id=1, source_target_pairs={{1,0},{2,1},{3,2},{4,3},{5,4},{14,15},{13,14},{12,13},{11,12},{10,... | collective-permute-start | bytes 1572872 | tf_op jit(solution)/shard_map/ppermute | solution.py:26
  63.0 2.8 %collective-permute-start.5 = (bf16[512,512]{1,0:T(8,128)(2,1)S(1)}, bf16[512,512]{1,0:T(8,128)(2,1)S(1)}, u32[]{:S(2)}, u32[]{:S(2)}) collective-permute-start(bf16[512,512]{1,0:T(8,128)(2,1)S(1)} %collective-permute-done.3.refs_4_), channel_id=1, source_target_pairs={{1,0},{2,1},{3,2},{4,3},{5,4},{14,15},{13,14},{12,13},{11,12},{10,... | collective-permute-start | bytes 1572872 | tf_op jit(solution)/shard_map/ppermute | solution.py:26
  63.7 2.9 %collective-permute-start.16 = (bf16[512,512]{1,0:T(8,128)(2,1)S(1)}, bf16[512,512]{1,0:T(8,128)(2,1)S(1)}, u32[]{:S(2)}, u32[]{:S(2)}) collective-permute-start(bf16[512,512]{1,0:T(8,128)(2,1)S(1)} %copy-done), channel_id=1, source_target_pairs={{0,1},{1,2},{2,3},{15,14},{14,13},{13,12},{16,17},{17,18},{18,19},... | collective-permute-start | bytes 1572872 | tf_op jit(solution)/shard_map/ppermute | solution.py:30
  64.4 2.9 %collective-permute-start.13 = (bf16[512,512]{1,0:T(8,128)(2,1)}, bf16[512,512]{1,0:T(8,128)(2,1)S(1)}, u32[]{:S(2)}, u32[]{:S(2)}) collective-permute-start(bf16[512,512]{1,0:T(8,128)(2,1)} %early_tokens.1.refs_0_), channel_id=1, source_target_pairs={{0,1},{1,2},{2,3},{15,14},{14,13},{13,12},{16,17},{17,18},{18,19},... | collective-permute-start | bytes 1572872 | tf_op jit(solution)/shard_map/ppermute | solution.py:30
  65.1 3.6 %collective-permute-start.8 = (bf16[512,512]{1,0:T(8,128)(2,1)S(1)}, bf16[512,512]{1,0:T(8,128)(2,1)S(1)}, u32[]{:S(2)}, u32[]{:S(2)}) collective-permute-start(bf16[512,512]{1,0:T(8,128)(2,1)S(1)} %collective-permute-done.6.refs_7_), channel_id=1, source_target_pairs={{1,0},{2,1},{3,2},{4,3},{14,15},{13,14},{12,13},{11,12},{17,16},{1... | collective-permute-start | bytes 1572872 | tf_op jit(solution)/shard_map/ppermute | solution.py:26
  65.9 4.4 %collective-permute-start.7 = (bf16[512,512]{1,0:T(8,128)(2,1)S(1)}, bf16[512,512]{1,0:T(8,128)(2,1)S(1)}, u32[]{:S(2)}, u32[]{:S(2)}) collective-permute-start(bf16[512,512]{1,0:T(8,128)(2,1)S(1)} %collective-permute-done.5.refs_6_), channel_id=1, source_target_pairs={{1,0},{2,1},{3,2},{4,3},{14,15},{13,14},{12,13},{11,12},{17,16},{1... | collective-permute-start | bytes 1572872 | tf_op jit(solution)/shard_map/ppermute | solution.py:26
  66.6 5.2 %collective-permute-start.17 = (bf16[512,512]{1,0:T(8,128)(2,1)S(1)}, bf16[512,512]{1,0:T(8,128)(2,1)S(1)}, u32[]{:S(2)}, u32[]{:S(2)}) collective-permute-start(bf16[512,512]{1,0:T(8,128)(2,1)S(1)} %collective-permute-done.16.refs_9_.refs_21_), channel_id=1, source_target_pairs={{1,2},{2,3},{14,13},{13,12},{17,18},{18,19},{30,29},{29,28},{33,34... | collective-permute-start | bytes 1572872 | tf_op jit(solution)/shard_map/ppermute | solution.py:30
  67.3 5.9 %collective-permute-start.14 = (bf16[512,512]{1,0:T(8,128)(2,1)S(1)}, bf16[512,512]{1,0:T(8,128)(2,1)}, u32[]{:S(2)}, u32[]{:S(2)}) collective-permute-start(bf16[512,512]{1,0:T(8,128)(2,1)S(1)} %collective-permute-done.13.refs_8_.refs_20_), channel_id=1, source_target_pairs={{1,2},{2,3},{14,13},{13,12},{17,18},{18,19},{30,29},{29,28},{33,34... | collective-permute-start | bytes 1572872 | tf_op jit(solution)/shard_map/ppermute | solution.py:30
  68.8 5.9 %collective-permute-start.10 = (bf16[512,512]{1,0:T(8,128)(2,1)S(1)}, bf16[512,512]{1,0:T(8,128)(2,1)}, u32[]{:S(2)}, u32[]{:S(2)}) collective-permute-start(bf16[512,512]{1,0:T(8,128)(2,1)S(1)} %collective-permute-done.8.refs_9_), channel_id=1, source_target_pairs={{1,0},{2,1},{3,2},{14,15},{13,14},{12,13},{17,16},{18,17},{19,18},... | collective-permute-start | bytes 1572872 | tf_op jit(solution)/shard_map/ppermute | solution.py:26
  70.3 5.9 %collective-permute-start.9 = (bf16[512,512]{1,0:T(8,128)(2,1)S(1)}, bf16[512,512]{1,0:T(8,128)(2,1)}, u32[]{:S(2)}, u32[]{:S(2)}) collective-permute-start(bf16[512,512]{1,0:T(8,128)(2,1)S(1)} %collective-permute-done.7.refs_8_), channel_id=1, source_target_pairs={{1,0},{2,1},{3,2},{14,15},{13,14},{12,13},{17,16},{18,17},{19,18},... | collective-permute-start | bytes 1572872 | tf_op jit(solution)/shard_map/ppermute | solution.py:26
  71.8 47.8 %collective-permute-start.18 = (bf16[512,512]{1,0:T(8,128)(2,1)S(1)}, bf16[512,512]{1,0:T(8,128)(2,1)}, u32[]{:S(2)}, u32[]{:S(2)}) collective-permute-start(bf16[512,512]{1,0:T(8,128)(2,1)S(1)} %collective-permute-done.17.refs_7_.refs_17_), channel_id=1, source_target_pairs={{2,3},{13,12},{18,19},{29,28},{34,35},{45,44},{50,51},{61,60},{66,... | collective-permute-start | bytes 1572872 | tf_op jit(solution)/shard_map/ppermute | solution.py:30
  73.2 46.3 %collective-permute-start.15 = (bf16[512,512]{1,0:T(8,128)(2,1)}, bf16[512,512]{1,0:T(8,128)(2,1)}, u32[]{:S(2)}, u32[]{:S(2)}) collective-permute-start(bf16[512,512]{1,0:T(8,128)(2,1)} %collective-permute-done.14.refs_6_.refs_16_), channel_id=1, source_target_pairs={{2,3},{13,12},{18,19},{29,28},{34,35},{45,44},{50,51},{61,60},{66,... | collective-permute-start | bytes 1572872 | tf_op jit(solution)/shard_map/ppermute | solution.py:30
  74.7 44.9 %collective-permute-start.12 = (bf16[512,512]{1,0:T(8,128)(2,1)}, bf16[512,512]{1,0:T(8,128)(2,1)}, u32[]{:S(2)}, u32[]{:S(2)}) collective-permute-start(bf16[512,512]{1,0:T(8,128)(2,1)} %collective-permute-done.10.refs_1_.refs_11_), channel_id=1, source_target_pairs={{1,0},{2,1},{14,15},{13,14},{17,16},{18,17},{30,31},{29,30},{33,32... | collective-permute-start | bytes 1572872 | tf_op jit(solution)/shard_map/ppermute | solution.py:26
  76.1 43.4 %collective-permute-start.11 = (bf16[512,512]{1,0:T(8,128)(2,1)}, bf16[512,512]{1,0:T(8,128)(2,1)}, u32[]{:S(2)}, u32[]{:S(2)}) collective-permute-start(bf16[512,512]{1,0:T(8,128)(2,1)} %collective-permute-done.9.refs_0_.refs_10_), channel_id=1, source_target_pairs={{1,0},{2,1},{14,15},{13,14},{17,16},{18,17},{30,31},{29,30},{33,32... | collective-permute-start | bytes 1572872 | tf_op jit(solution)/shard_map/ppermute | solution.py:26
  119.6 5.1 %collective-permute-start.19 = (bf16[512,512]{1,0:T(8,128)(2,1)}, bf16[512,512]{1,0:T(8,128)(2,1)S(1)}, u32[]{:S(2)}, u32[]{:S(2)}) collective-permute-start(bf16[512,512]{1,0:T(8,128)(2,1)} %collective-permute-done.11.refs_4_.refs_14_), channel_id=1, source_target_pairs={{1,0},{14,15},{17,16},{30,31},{33,32},{46,47},{49,48},{62,63},{65,... | collective-permute-start | bytes 1572872 | tf_op jit(solution)/shard_map/ppermute | solution.py:26
  120.3 4.4 %collective-permute-start.20 = (bf16[512,512]{1,0:T(8,128)(2,1)}, bf16[512,512]{1,0:T(8,128)(2,1)S(1)}, u32[]{:S(2)}, u32[]{:S(2)}) collective-permute-start(bf16[512,512]{1,0:T(8,128)(2,1)} %collective-permute-done.12.refs_5_.refs_15_), channel_id=1, source_target_pairs={{1,0},{14,15},{17,16},{30,31},{33,32},{46,47},{49,48},{62,63},{65,... | collective-permute-start | bytes 1572872 | tf_op jit(solution)/shard_map/ppermute | solution.py:26
  123.4 61.4 %collective-permute-start.22 = (bf16[1024,512]{1,0:T(8,128)(2,1)}, bf16[1024,512]{1,0:T(8,128)(2,1)S(1)}, u32[]{:S(2)}, u32[]{:S(2)}) collective-permute-start(bf16[1024,512]{1,0:T(8,128)(2,1)} %get-tuple-element.44), channel_id=1, source_target_pairs={{1,5},{2,6},{3,7},{14,10},{13,9},{12,8},{17,21},{18,22},{19,23},{3... | collective-permute-start | bytes 3145736 | tf_op jit(solution)/shard_map/ppermute | solution.py:34
  127.4 57.4 %collective-permute-start.21 = (bf16[1024,512]{1,0:T(8,128)(2,1)}, bf16[1024,512]{1,0:T(8,128)(2,1)S(1)}, u32[]{:S(2)}, u32[]{:S(2)}) collective-permute-start(bf16[1024,512]{1,0:T(8,128)(2,1)} %partner_last.1), channel_id=1, source_target_pairs={{0,4},{15,11},{16,20},{31,27},{32,36},{47,43},{48,52},{63,59},{64,... | collective-permute-start | bytes 3145736 | tf_op jit(solution)/shard_map/ppermute | solution.py:34
  (16 other events, 413.9 us)
Sparse Core Ops, SparseCore 0:
  44.6 72.6 all-gather.1

commit v4 on v3

--- a/solution.py
+++ b/solution.py
@@ -290,10 +290,11 @@
         (2, [(6, sixth), (-2, back[2])]),
         (None, [(-1, back[1])]),
     ]
-    total, ready = project(far, place, weights, 1, total, kinds, "partner_far")
+    (ready,) = project(far, place, weights, 1, total, kinds[1:], "partner_far")
     sent_first = deliver(ready, (1, 2, 3))
-    last, total = in_order((came[7], total))
-    (ready,) = project([(None, [(7, last)])], place, weights, 1, total, kinds[1:], "partner_last")
+    last, total, _ = in_order((came[7], total, ready))
+    end = [(None, [(5, fifth)]), (None, [(6, sixth)]), (None, [(7, last)])]
+    (ready,) = project(end, place, weights, 1, total, kinds[1:], "partner_last")
     sent_last = deliver(ready, (0,))
 
     every = near + far[:2] + [(1, [(7, last), (-1, back[1])])]

time: 194 us -> 194 us (level)
  starting transfers between devices: 29.8 us -> 27.5 us
  waiting for transfers between devices: 100 us -> 102 us
    ppermute x14, starting transfers between devices: 16.7 us -> 13.6 us  [inward(): lax.ppermute(block, LINE, on_line([(u, u - 1) for u in range(1, LINE_LEN...]
    all_gather x1, waiting for transfers between devices: 39.7 us -> 42 us  [per_device(): weights = lax.all_gather(shard, PLANE, axis=0, tiled=True)]
where the time goes in v4:
time: 194 us; the launch traced here: 193 us
  waiting for transfers between devices  102 us (53%)
  starting transfers between devices  27.5 us (14%)
  blocking collectives  26.9 us (14%)
  Pallas kernels  18.6 us (10%)
  between operations  13.9 us (7%)
  other arithmetic  2.89 us (1%)
    ppermute x2, waiting for transfers between devices, deliver(): lax.ppermute(block, LINE, on_line([(u, u + WORKERS) for u in workers]))  54.1 us
    all_gather x1, waiting for transfers between devices, per_device(): weights = lax.all_gather(shard, PLANE, axis=0, tiled=True)  42 us
    all_gather x1, blocking collectives, per_device(): shard = lax.all_gather(own_shard, ('zh', 'th'), axis=0, tiled=True)  26.9 us
    ppermute x14, starting transfers between devices, inward(): lax.ppermute(block, LINE, on_line([(u, u - 1) for u in range(1, LINE_LEN...  13.6 us
    pallas_call x2, Pallas kernels, local_part(): pl.pallas_call(functools.partial(local_kernel, late), in_specs=[pl.BlockS...  11.1 us
    pallas_call x4, Pallas kernels, project(): pl.pallas_call(functools.partial(project_kernel, shape_of_slots, side, le...  7.54 us
    ppermute x6, starting transfers between devices, outward(): lax.ppermute(block, LINE, on_line([(u, u + 1) for u in range(step - 1, WO...  7.25 us
    ppermute x14, waiting for transfers between devices, inward(): lax.ppermute(block, LINE, on_line([(u, u - 1) for u in range(1, LINE_LEN...  5.7 us
  transfers between devices with their start and end apart: 24, of which 3 were waited for; matrix products, arithmetic and copies ran while one was open for 0% of the time, Pallas kernels for 7%

profile of v4, /device:TPU:1, one launch (start us, length us, event | category | flops | bytes accessed | tf_op | source)
XLA Modules:
  0.0 193.3 jit_solution(14025936126433607991)
XLA Ops:
  6.5 5.7 %late_tokens.1 = (bf16[512,512]{1,0:T(8,128)(2,1)}, bf16[160,512]{1,0:T(8,128)(2,1)}) custom-call(bf16[3,1024,512]{2,1,0:T(8,128)(2,1)} %x_ref.2, f32[3,3,512]{2,1,0:T(4,128)} %taps_ref.3, bf16[4,8,128]{2,1,0:T(8,128)(2,1)} %bitcast.10, bf16[4,8,128]{2,1,0:T(8,128)(2,1)} %bitcast.11), custom_call_target="tpu_custom_call" | custom-call | flops 1073741824 | bytes 4194304 | tf_op jit(solution)/shard_map/late_tokens/pallas_call | solution.py:133
  12.3 4.6 %collective-permute-start = (bf16[160,512]{1,0:T(8,128)(2,1)}, bf16[160,512]{1,0:T(8,128)(2,1)S(1)}, u32[]{:S(2)}, u32[]{:S(2)}) collective-permute-start(bf16[160,512]{1,0:T(8,128)(2,1)} %get-tuple-element.26), channel_id=1, source_target_pairs={{0,8},{8,16},{16,24},{24,32},{32,40},{40,48},{48,56},{56,64},{64,7... | collective-permute-start | bytes 491528 | tf_op jit(solution)/shard_map/ppermute | solution.py:259
  17.5 26.9 %all_gather.6 = bf16[256,512]{1,0:T(8,128)(2,1)} all-gather(bf16[64,512]{1,0:T(8,128)(2,1)S(1)} %copy-done.17), channel_id=1, replica_groups=mesh['zh'=2,'y'=4,'x'=4,'c'=2,'th'=2,'tl'=4] {'zh','th'}, dimensions={0}, use_global_device_ids=true | all-gather | bytes 327680 | tf_op jit(solution)/shard_map/all_gather | solution.py:262
  44.4 2.6 %collective-permute-start.2 = (bf16[512,512]{1,0:T(8,128)(2,1)}, bf16[512,512]{1,0:T(8,128)(2,1)S(1)}, u32[]{:S(2)}, u32[]{:S(2)}) collective-permute-start(bf16[512,512]{1,0:T(8,128)(2,1)} %get-tuple-element.24.refs_1_), channel_id=1, source_target_pairs={{1,0},{2,1},{3,2},{4,3},{5,4},{6,5},{7,6},{14,15},{13,14},{12,13},... | collective-permute-start | bytes 1572872 | tf_op jit(solution)/shard_map/ppermute | solution.py:26
  47.0 5.4 %early_tokens.1.refs_0_ = bf16[512,512]{1,0:T(8,128)(2,1)} custom-call(bf16[3,1024,512]{2,1,0:T(8,128)(2,1)} %x_ref.2, f32[3,3,512]{2,1,0:T(4,128)} %taps_ref.3, bf16[4,8,128]{2,1,0:T(8,128)(2,1)} %bitcast.12, bf16[160,512]{1,0:T(8,128)(2,1)} %copy-done.18), custom_call_target="tpu_custom_call" | custom-call | flops 1073741824 | bytes 4194304 | tf_op jit(solution)/shard_map/early_tokens/pallas_call | solution.py:133
  52.4 2.6 %collective-permute-start.1 = (bf16[512,512]{1,0:T(8,128)(2,1)}, bf16[512,512]{1,0:T(8,128)(2,1)S(1)}, u32[]{:S(2)}, u32[]{:S(2)}) collective-permute-start(bf16[512,512]{1,0:T(8,128)(2,1)} %early_tokens.1.refs_0_), channel_id=1, source_target_pairs={{1,0},{2,1},{3,2},{4,3},{5,4},{6,5},{7,6},{14,15},{13,14},{12,13},... | collective-permute-start | bytes 1572872 | tf_op jit(solution)/shard_map/ppermute | solution.py:26
  55.8 5.7 %collective-permute-done.1.refs_2_ = bf16[512,512]{1,0:T(8,128)(2,1)S(1)} collective-permute-done((bf16[512,512]{1,0:T(8,128)(2,1)}, bf16[512,512]{1,0:T(8,128)(2,1)S(1)}, u32[]{:S(2)}, u32[]{:S(2)}) %collective-permute-start.1) | collective-permute-done | bytes 524320 | tf_op jit(solution)/shard_map/ppermute | solution.py:26
  62.9 0.7 collective-permute-start.5
  65.8 0.7 collective-permute-start.7
  66.5 1.5 collective-permute-start.17
  68.0 1.4 collective-permute-start.14
  70.9 1.5 collective-permute-start.18
  72.4 1.4 collective-permute-start.15
  75.3 42.0 %all-gather.2.cloned.1.call-done = bf16[8192,512]{1,0:T(8,128)(2,1)} async-done(((bf16[256,512]{1,0:T(8,128)(2,1)}), bf16[8192,512]{1,0:T(8,128)(2,1)}) %all-gather.2.cloned.1.call-update) | async-done | bytes 8388624 | tf_op jit(solution)/shard_map/all_gather | solution.py:264
  117.3 2.1 %partner_near.1.refs_11_.refs_7_ = f32[1024,512]{1,0:T(8,128)} custom-call(s32[4]{0:T(128)} %pad_add_fusion.place_ref, bf16[512,512]{1,0:T(8,128)(2,1)} %early_tokens.1.refs_0_, bf16[512,512]{1,0:T(8,128)(2,1)} %get-tuple-element.24.refs_1_, bf16[512,512]{1,0:T(8,128)(2,1)} %copy-done.6, bf16[512,512]{1,0:T(8,128)(2,1)} %copy-done.5, ...), custom_call_target="tpu_custom_call" | custom-call | flops 524288 | bytes 524288 | tf_op jit(solution)/shard_map/partner_near/pallas_call | solution.py:224
  120.9 1.8 partner_far.1
  122.7 1.3 collective-permute-start.22
  124.0 0.8 copy-done.15
  124.9 0.8 copy-done.16
  125.7 1.7 partner_last.1
  127.4 0.7 collective-permute-start.21
  128.2 1.9 own_columns.1
  130.1 54.1 %collective-permute-done.22 = bf16[1024,512]{1,0:T(8,128)(2,1)} collective-permute-done((bf16[1024,512]{1,0:T(8,128)(2,1)}, bf16[1024,512]{1,0:T(8,128)(2,1)}, u32[]{:S(2)}, u32[]{:S(2)}) %collective-permute-start.22) | collective-permute-done | bytes 1048608 | tf_op jit(solution)/shard_map/ppermute | solution.py:34
  184.1 2.3 %select_select_fusion = bf16[1024,512]{1,0:T(8,128)(2,1)} fusion(bf16[1024,512]{1,0:T(8,128)(2,1)} %own_columns.1, bf16[1024,512]{1,0:T(8,128)(2,1)S(1)} %collective-permute-done.21, bf16[1024,512]{1,0:T(8,128)(2,1)} %collective-permute-done.22, pred[]{:T(512)S(6)} %eq.8, pred[]{:T(512)S(6)} %lt.3), kind=kLoop, calls=%fused_computation | loop fusion | flops 1048576 | bytes 4194306 | tf_op jit(solution)/shard_map/jit(_where)/select_n | solution.py:303
  (72 shorter events, 9.0 us)
Async XLA Ops:
  6.5 110.7 %all-gather.2.cloned.1.call-start = ((), (), s32[]{:S(2)}) async-start(), calls=%async_computation | async-start | bytes 8650752 | tf_op jit(solution)/shard_map/all_gather | solution.py:264
  12.3 32.1 %collective-permute-start = (bf16[160,512]{1,0:T(8,128)(2,1)}, bf16[160,512]{1,0:T(8,128)(2,1)S(1)}, u32[]{:S(2)}, u32[]{:S(2)}) collective-permute-start(bf16[160,512]{1,0:T(8,128)(2,1)} %get-tuple-element.26), channel_id=1, source_target_pairs={{0,8},{8,16},{16,24},{24,32},{32,40},{40,48},{48,56},{56,64},{64,7... | collective-permute-start | bytes 491528 | tf_op jit(solution)/shard_map/ppermute | solution.py:259
  44.4 10.7 %collective-permute-start.2 = (bf16[512,512]{1,0:T(8,128)(2,1)}, bf16[512,512]{1,0:T(8,128)(2,1)S(1)}, u32[]{:S(2)}, u32[]{:S(2)}) collective-permute-start(bf16[512,512]{1,0:T(8,128)(2,1)} %get-tuple-element.24.refs_1_), channel_id=1, source_target_pairs={{1,0},{2,1},{3,2},{4,3},{5,4},{6,5},{7,6},{14,15},{13,14},{12,13},... | collective-permute-start | bytes 1572872 | tf_op jit(solution)/shard_map/ppermute | solution.py:26
  52.4 9.0 %collective-permute-start.1 = (bf16[512,512]{1,0:T(8,128)(2,1)}, bf16[512,512]{1,0:T(8,128)(2,1)S(1)}, u32[]{:S(2)}, u32[]{:S(2)}) collective-permute-start(bf16[512,512]{1,0:T(8,128)(2,1)} %early_tokens.1.refs_0_), channel_id=1, source_target_pairs={{1,0},{2,1},{3,2},{4,3},{5,4},{6,5},{7,6},{14,15},{13,14},{12,13},... | collective-permute-start | bytes 1572872 | tf_op jit(solution)/shard_map/ppermute | solution.py:26
  55.1 7.1 %collective-permute-start.4 = (bf16[512,512]{1,0:T(8,128)(2,1)S(1)}, bf16[512,512]{1,0:T(8,128)(2,1)S(1)}, u32[]{:S(2)}, u32[]{:S(2)}) collective-permute-start(bf16[512,512]{1,0:T(8,128)(2,1)S(1)} %collective-permute-done.2.refs_3_), channel_id=1, source_target_pairs={{1,0},{2,1},{3,2},{4,3},{5,4},{6,5},{14,15},{13,14},{12,13},{11,12... | collective-permute-start | bytes 1572872 | tf_op jit(solution)/shard_map/ppermute | solution.py:26
  61.5 1.4 collective-permute-start.3
  62.2 2.8 %collective-permute-start.6 = (bf16[512,512]{1,0:T(8,128)(2,1)S(1)}, bf16[512,512]{1,0:T(8,128)(2,1)S(1)}, u32[]{:S(2)}, u32[]{:S(2)}) collective-permute-start(bf16[512,512]{1,0:T(8,128)(2,1)S(1)} %collective-permute-done.4.refs_5_), channel_id=1, source_target_pairs={{1,0},{2,1},{3,2},{4,3},{5,4},{14,15},{13,14},{12,13},{11,12},{10,... | collective-permute-start | bytes 1572872 | tf_op jit(solution)/shard_map/ppermute | solution.py:26
  62.9 2.8 %collective-permute-start.5 = (bf16[512,512]{1,0:T(8,128)(2,1)S(1)}, bf16[512,512]{1,0:T(8,128)(2,1)S(1)}, u32[]{:S(2)}, u32[]{:S(2)}) collective-permute-start(bf16[512,512]{1,0:T(8,128)(2,1)S(1)} %collective-permute-done.3.refs_4_), channel_id=1, source_target_pairs={{1,0},{2,1},{3,2},{4,3},{5,4},{14,15},{13,14},{12,13},{11,12},{10,... | collective-permute-start | bytes 1572872 | tf_op jit(solution)/shard_map/ppermute | solution.py:26
  63.6 2.9 %collective-permute-start.16 = (bf16[512,512]{1,0:T(8,128)(2,1)S(1)}, bf16[512,512]{1,0:T(8,128)(2,1)S(1)}, u32[]{:S(2)}, u32[]{:S(2)}) collective-permute-start(bf16[512,512]{1,0:T(8,128)(2,1)S(1)} %copy-done.4), channel_id=1, source_target_pairs={{0,1},{1,2},{2,3},{15,14},{14,13},{13,12},{16,17},{17,18},{18,19},... | collective-permute-start | bytes 1572872 | tf_op jit(solution)/shard_map/ppermute | solution.py:30
  64.3 3.6 %collective-permute-start.13 = (bf16[512,512]{1,0:T(8,128)(2,1)}, bf16[512,512]{1,0:T(8,128)(2,1)S(1)}, u32[]{:S(2)}, u32[]{:S(2)}) collective-permute-start(bf16[512,512]{1,0:T(8,128)(2,1)} %early_tokens.1.refs_0_), channel_id=1, source_target_pairs={{0,1},{1,2},{2,3},{15,14},{14,13},{13,12},{16,17},{17,18},{18,19},... | collective-permute-start | bytes 1572872 | tf_op jit(solution)/shard_map/ppermute | solution.py:30
  65.1 4.4 %collective-permute-start.8 = (bf16[512,512]{1,0:T(8,128)(2,1)S(1)}, bf16[512,512]{1,0:T(8,128)(2,1)S(1)}, u32[]{:S(2)}, u32[]{:S(2)}) collective-permute-start(bf16[512,512]{1,0:T(8,128)(2,1)S(1)} %collective-permute-done.6.refs_7_), channel_id=1, source_target_pairs={{1,0},{2,1},{3,2},{4,3},{14,15},{13,14},{12,13},{11,12},{17,16},{1... | collective-permute-start | bytes 1572872 | tf_op jit(solution)/shard_map/ppermute | solution.py:26
  65.8 4.3 %collective-permute-start.7 = (bf16[512,512]{1,0:T(8,128)(2,1)S(1)}, bf16[512,512]{1,0:T(8,128)(2,1)S(1)}, u32[]{:S(2)}, u32[]{:S(2)}) collective-permute-start(bf16[512,512]{1,0:T(8,128)(2,1)S(1)} %collective-permute-done.5.refs_6_), channel_id=1, source_target_pairs={{1,0},{2,1},{3,2},{4,3},{14,15},{13,14},{12,13},{11,12},{17,16},{1... | collective-permute-start | bytes 1572872 | tf_op jit(solution)/shard_map/ppermute | solution.py:26
  66.5 4.3 %collective-permute-start.17 = (bf16[512,512]{1,0:T(8,128)(2,1)S(1)}, bf16[512,512]{1,0:T(8,128)(2,1)}, u32[]{:S(2)}, u32[]{:S(2)}) collective-permute-start(bf16[512,512]{1,0:T(8,128)(2,1)S(1)} %collective-permute-done.16.refs_9_.refs_21_), channel_id=1, source_target_pairs={{1,2},{2,3},{14,13},{13,12},{17,18},{18,19},{30,29},{29,28},{33,34... | collective-permute-start | bytes 1572872 | tf_op jit(solution)/shard_map/ppermute | solution.py:30
  68.0 4.4 %collective-permute-start.14 = (bf16[512,512]{1,0:T(8,128)(2,1)S(1)}, bf16[512,512]{1,0:T(8,128)(2,1)}, u32[]{:S(2)}, u32[]{:S(2)}) collective-permute-start(bf16[512,512]{1,0:T(8,128)(2,1)S(1)} %collective-permute-done.13.refs_8_.refs_20_), channel_id=1, source_target_pairs={{1,2},{2,3},{14,13},{13,12},{17,18},{18,19},{30,29},{29,28},{33,34... | collective-permute-start | bytes 1572872 | tf_op jit(solution)/shard_map/ppermute | solution.py:30
  69.4 4.4 %collective-permute-start.10 = (bf16[512,512]{1,0:T(8,128)(2,1)S(1)}, bf16[512,512]{1,0:T(8,128)(2,1)S(1)}, u32[]{:S(2)}, u32[]{:S(2)}) collective-permute-start(bf16[512,512]{1,0:T(8,128)(2,1)S(1)} %collective-permute-done.8.refs_9_), channel_id=1, source_target_pairs={{1,0},{2,1},{3,2},{14,15},{13,14},{12,13},{17,16},{18,17},{19,18},... | collective-permute-start | bytes 1572872 | tf_op jit(solution)/shard_map/ppermute | solution.py:26
  70.1 4.4 %collective-permute-start.9 = (bf16[512,512]{1,0:T(8,128)(2,1)S(1)}, bf16[512,512]{1,0:T(8,128)(2,1)S(1)}, u32[]{:S(2)}, u32[]{:S(2)}) collective-permute-start(bf16[512,512]{1,0:T(8,128)(2,1)S(1)} %collective-permute-done.7.refs_8_), channel_id=1, source_target_pairs={{1,0},{2,1},{3,2},{14,15},{13,14},{12,13},{17,16},{18,17},{19,18},... | collective-permute-start | bytes 1572872 | tf_op jit(solution)/shard_map/ppermute | solution.py:26
  70.9 48.6 %collective-permute-start.18 = (bf16[512,512]{1,0:T(8,128)(2,1)}, bf16[512,512]{1,0:T(8,128)(2,1)}, u32[]{:S(2)}, u32[]{:S(2)}) collective-permute-start(bf16[512,512]{1,0:T(8,128)(2,1)} %collective-permute-done.17.refs_7_.refs_17_), channel_id=1, source_target_pairs={{2,3},{13,12},{18,19},{29,28},{34,35},{45,44},{50,51},{61,60},{66,... | collective-permute-start | bytes 1572872 | tf_op jit(solution)/shard_map/ppermute | solution.py:30
  72.4 47.1 %collective-permute-start.15 = (bf16[512,512]{1,0:T(8,128)(2,1)}, bf16[512,512]{1,0:T(8,128)(2,1)}, u32[]{:S(2)}, u32[]{:S(2)}) collective-permute-start(bf16[512,512]{1,0:T(8,128)(2,1)} %collective-permute-done.14.refs_6_.refs_16_), channel_id=1, source_target_pairs={{2,3},{13,12},{18,19},{29,28},{34,35},{45,44},{50,51},{61,60},{66,... | collective-permute-start | bytes 1572872 | tf_op jit(solution)/shard_map/ppermute | solution.py:30
  73.8 45.6 %collective-permute-start.12 = (bf16[512,512]{1,0:T(8,128)(2,1)S(1)}, bf16[512,512]{1,0:T(8,128)(2,1)S(1)}, u32[]{:S(2)}, u32[]{:S(2)}) collective-permute-start(bf16[512,512]{1,0:T(8,128)(2,1)S(1)} %collective-permute-done.10.refs_1_.refs_11_), channel_id=1, source_target_pairs={{1,0},{2,1},{14,15},{13,14},{17,16},{18,17},{30,31},{29,30},{33,32... | collective-permute-start | bytes 1572872 | tf_op jit(solution)/shard_map/ppermute | solution.py:26
  74.6 44.9 %collective-permute-start.11 = (bf16[512,512]{1,0:T(8,128)(2,1)S(1)}, bf16[512,512]{1,0:T(8,128)(2,1)S(1)}, u32[]{:S(2)}, u32[]{:S(2)}) collective-permute-start(bf16[512,512]{1,0:T(8,128)(2,1)S(1)} %collective-permute-done.9.refs_0_.refs_10_), channel_id=1, source_target_pairs={{1,0},{2,1},{14,15},{13,14},{17,16},{18,17},{30,31},{29,30},{33,32... | collective-permute-start | bytes 1572872 | tf_op jit(solution)/shard_map/ppermute | solution.py:26
  119.5 4.5 %collective-permute-start.19 = (bf16[512,512]{1,0:T(8,128)(2,1)S(1)}, bf16[512,512]{1,0:T(8,128)(2,1)S(1)}, u32[]{:S(2)}, u32[]{:S(2)}) collective-permute-start(bf16[512,512]{1,0:T(8,128)(2,1)S(1)} %collective-permute-done.11.refs_4_.refs_14_.refs_2_), channel_id=1, source_target_pairs={{1,0},{14,15},{17,16},{30,31},{33,32},{46,47},{49,48},{62,63},{65,... | collective-permute-start | bytes 1572872 | tf_op jit(solution)/shard_map/ppermute | solution.py:26
  120.2 3.8 %collective-permute-start.20 = (bf16[512,512]{1,0:T(8,128)(2,1)S(1)}, bf16[512,512]{1,0:T(8,128)(2,1)S(1)}, u32[]{:S(2)}, u32[]{:S(2)}) collective-permute-start(bf16[512,512]{1,0:T(8,128)(2,1)S(1)} %collective-permute-done.12.refs_5_.refs_15_.refs_3_), channel_id=1, source_target_pairs={{1,0},{14,15},{17,16},{30,31},{33,32},{46,47},{49,48},{62,63},{65,... | collective-permute-start | bytes 1572872 | tf_op jit(solution)/shard_map/ppermute | solution.py:26
  122.7 61.4 %collective-permute-start.22 = (bf16[1024,512]{1,0:T(8,128)(2,1)}, bf16[1024,512]{1,0:T(8,128)(2,1)}, u32[]{:S(2)}, u32[]{:S(2)}) collective-permute-start(bf16[1024,512]{1,0:T(8,128)(2,1)} %partner_far.1), channel_id=1, source_target_pairs={{1,5},{2,6},{3,7},{14,10},{13,9},{12,8},{17,21},{18,22},{19,23},{3... | collective-permute-start | bytes 3145736 | tf_op jit(solution)/shard_map/ppermute | solution.py:34
  127.4 56.7 %collective-permute-start.21 = (bf16[1024,512]{1,0:T(8,128)(2,1)}, bf16[1024,512]{1,0:T(8,128)(2,1)S(1)}, u32[]{:S(2)}, u32[]{:S(2)}) collective-permute-start(bf16[1024,512]{1,0:T(8,128)(2,1)} %partner_last.1), channel_id=1, source_target_pairs={{0,4},{15,11},{16,20},{31,27},{32,36},{47,43},{48,52},{63,59},{64,... | collective-permute-start | bytes 3145736 | tf_op jit(solution)/shard_map/ppermute | solution.py:34
  (19 other events, 339.2 us)
Sparse Core Ops, SparseCore 0:
  44.5 72.6 all-gather.1

commit v5 on v3

--- a/solution.py
+++ b/solution.py
@@ -279,26 +279,21 @@
             back.append(tuple(outward(part, step - 2) for part in back[-1]))
 
     kinds = (jnp.float32, jnp.bfloat16)
-    near = [(None, [(d, came[d])]) for d in range(5)]
-    (total,) = project(near, place, weights, 1, None, kinds[:1], "partner_near")
-    fifth = came[5]
-    came.append(tuple(inward(part, LINE_LEN - 2) for part in fifth))
-    sixth, total, back[3] = in_order((came[6], total, back[3]))
+    near = [(None, [(d, came[d])]) for d in range(5)] + [(3, [(5, came[5]), (-3, back[3])])]
+    came.append(tuple(inward(part, LINE_LEN - 2) for part in came[5]))
+    slots = near + [(None, [(-2, back[2])]), (None, [(-1, back[1])])]
+    total, ready = project(slots, place, weights, 1, None, kinds, "partner_first")
+    sent_first = deliver(ready, (2, 3))
+    sixth, total = in_order((came[6], total))
     came.append(tuple(inward(part, LINE_LEN - 1) for part in sixth))
-    far = [
-        (3, [(5, fifth), (-3, back[3])]),
-        (2, [(6, sixth), (-2, back[2])]),
-        (None, [(-1, back[1])]),
-    ]
-    total, ready = project(far, place, weights, 1, total, kinds, "partner_far")
-    sent_first = deliver(ready, (1, 2, 3))
     last, total = in_order((came[7], total))
-    (ready,) = project([(None, [(7, last)])], place, weights, 1, total, kinds[1:], "partner_last")
-    sent_last = deliver(ready, (0,))
-
-    every = near + far[:2] + [(1, [(7, last), (-1, back[1])])]
+    slots = [(None, [(6, sixth)]), (None, [(7, last)])]
+    (ready,) = project(slots, place, weights, 1, total, kinds[1:], "partner_last")
+    sent_last = deliver(ready, (0, 1))
+
+    every = near + [(2, [(6, sixth), (-2, back[2])]), (1, [(7, last), (-1, back[1])])]
     (mine,) = project(every, place, weights, 0, None, kinds[1:], "own_columns")
-    given = jnp.where(u == WORKERS, sent_last, sent_first)
+    given = jnp.where(u < WORKERS + 2, sent_last, sent_first)
     return jnp.where(u < WORKERS, mine, given)
 
 

time: 194 us -> 195 us (level)
  the two profiles are of different devices: /device:TPU:1 before, /device:TPU:31 now
where the time goes in v5:
time: 195 us; the launch traced here: 194 us
  waiting for transfers between devices  94.9 us (49%)
  starting transfers between devices  41.1 us (21%)
  blocking collectives  23.2 us (12%)
  Pallas kernels  17.3 us (9%)
  between operations  13.9 us (7%)
  local copies, waits for them, and re-layouts  2.43 us (1%)
    ppermute x2, waiting for transfers between devices, deliver(): lax.ppermute(block, LINE, on_line([(u, u + WORKERS) for u in workers]))  61 us
    all_gather x1, waiting for transfers between devices, per_device(): weights = lax.all_gather(shard, PLANE, axis=0, tiled=True)  28.2 us
    all_gather x1, blocking collectives, per_device(): shard = lax.all_gather(own_shard, ('zh', 'th'), axis=0, tiled=True)  23.2 us
    ppermute x14, starting transfers between devices, inward(): lax.ppermute(block, LINE, on_line([(u, u - 1) for u in range(1, LINE_LEN...  18.4 us
    ppermute x1, starting transfers between devices, per_device(): halo = lax.ppermute(tail, SEQ, next_seq)  15.7 us
    pallas_call x2, Pallas kernels, local_part(): pl.pallas_call(functools.partial(local_kernel, late), in_specs=[pl.BlockS...  11.2 us
    pallas_call x3, Pallas kernels, project(): pl.pallas_call(functools.partial(project_kernel, shape_of_slots, side, le...  6.16 us
    ppermute x14, waiting for transfers between devices, inward(): lax.ppermute(block, LINE, on_line([(u, u - 1) for u in range(1, LINE_LEN...  5.7 us
  transfers between devices with their start and end apart: 24, of which 3 were waited for; matrix products, arithmetic and copies ran while one was open for 0% of the time, Pallas kernels for 6%

profile of v5, /device:TPU:31, one launch (start us, length us, event | category | flops | bytes accessed | tf_op | source)
XLA Modules:
  0.0 194.5 jit_solution(580657779968888939)
XLA Ops:
  6.5 5.7 %late_tokens.1 = (bf16[512,512]{1,0:T(8,128)(2,1)}, bf16[160,512]{1,0:T(8,128)(2,1)}) custom-call(bf16[3,1024,512]{2,1,0:T(8,128)(2,1)} %x_ref.2, f32[3,3,512]{2,1,0:T(4,128)} %taps_ref.3, bf16[4,8,128]{2,1,0:T(8,128)(2,1)} %bitcast.9, bf16[4,8,128]{2,1,0:T(8,128)(2,1)} %bitcast.10), custom_call_target="tpu_custom_call" | custom-call | flops 1073741824 | bytes 4194304 | tf_op jit(solution)/shard_map/late_tokens/pallas_call | solution.py:133
  12.3 15.7 %collective-permute-start = (bf16[160,512]{1,0:T(8,128)(2,1)}, bf16[160,512]{1,0:T(8,128)(2,1)S(1)}, u32[]{:S(2)}, u32[]{:S(2)}) collective-permute-start(bf16[160,512]{1,0:T(8,128)(2,1)} %get-tuple-element.26), channel_id=1, source_target_pairs={{0,8},{8,16},{16,24},{24,32},{32,40},{40,48},{48,56},{56,64},{64,7... | collective-permute-start | bytes 491528 | tf_op jit(solution)/shard_map/ppermute | solution.py:259
  28.6 23.2 %all_gather.6 = bf16[256,512]{1,0:T(8,128)(2,1)} all-gather(bf16[64,512]{1,0:T(8,128)(2,1)S(1)} %copy-done.16), channel_id=1, replica_groups=mesh['zh'=2,'y'=4,'x'=4,'c'=2,'th'=2,'tl'=4] {'zh','th'}, dimensions={0}, use_global_device_ids=true | all-gather | bytes 327680 | tf_op jit(solution)/shard_map/all_gather | solution.py:262
  51.8 3.3 %collective-permute-start.2 = (bf16[512,512]{1,0:T(8,128)(2,1)}, bf16[512,512]{1,0:T(8,128)(2,1)S(1)}, u32[]{:S(2)}, u32[]{:S(2)}) collective-permute-start(bf16[512,512]{1,0:T(8,128)(2,1)} %get-tuple-element.24.refs_1_), channel_id=1, source_target_pairs={{1,0},{2,1},{3,2},{4,3},{5,4},{6,5},{7,6},{14,15},{13,14},{12,13},... | collective-permute-start | bytes 1572872 | tf_op jit(solution)/shard_map/ppermute | solution.py:26
  55.1 5.4 %early_tokens.1.refs_0_ = bf16[512,512]{1,0:T(8,128)(2,1)} custom-call(bf16[3,1024,512]{2,1,0:T(8,128)(2,1)} %x_ref.2, f32[3,3,512]{2,1,0:T(4,128)} %taps_ref.3, bf16[4,8,128]{2,1,0:T(8,128)(2,1)} %bitcast.11, bf16[160,512]{1,0:T(8,128)(2,1)} %copy-done.17), custom_call_target="tpu_custom_call" | custom-call | flops 1073741824 | bytes 4194304 | tf_op jit(solution)/shard_map/early_tokens/pallas_call | solution.py:133
  60.6 3.8 %collective-permute-start.1 = (bf16[512,512]{1,0:T(8,128)(2,1)}, bf16[512,512]{1,0:T(8,128)(2,1)S(1)}, u32[]{:S(2)}, u32[]{:S(2)}) collective-permute-start(bf16[512,512]{1,0:T(8,128)(2,1)} %early_tokens.1.refs_0_), channel_id=1, source_target_pairs={{1,0},{2,1},{3,2},{4,3},{5,4},{6,5},{7,6},{14,15},{13,14},{12,13},... | collective-permute-start | bytes 1572872 | tf_op jit(solution)/shard_map/ppermute | solution.py:26
  65.1 5.7 %collective-permute-done.1.refs_2_ = bf16[512,512]{1,0:T(8,128)(2,1)S(1)} collective-permute-done((bf16[512,512]{1,0:T(8,128)(2,1)}, bf16[512,512]{1,0:T(8,128)(2,1)S(1)}, u32[]{:S(2)}, u32[]{:S(2)}) %collective-permute-start.1) | collective-permute-done | bytes 524320 | tf_op jit(solution)/shard_map/ppermute | solution.py:26
  72.2 0.7 collective-permute-start.5
  77.2 1.5 collective-permute-start.10
  78.7 1.5 collective-permute-start.9
  80.9 1.5 collective-permute-start.13
  82.3 1.4 collective-permute-start.18
  83.8 1.4 collective-permute-start.17
  85.2 0.8 copy-done.13
  86.1 28.2 %all-gather.2.cloned.1.call-done = bf16[8192,512]{1,0:T(8,128)(2,1)} async-done(((bf16[256,512]{1,0:T(8,128)(2,1)}), bf16[8192,512]{1,0:T(8,128)(2,1)}) %all-gather.2.cloned.1.call-update) | async-done | bytes 8388624 | tf_op jit(solution)/shard_map/all_gather | solution.py:264
  114.3 2.5 %partner_first.1 = (f32[1024,512]{1,0:T(8,128)}, bf16[1024,512]{1,0:T(8,128)(2,1)}) custom-call(s32[4]{0:T(128)} %pad_add_fusion.place_ref, bf16[512,512]{1,0:T(8,128)(2,1)} %early_tokens.1.refs_0_, bf16[512,512]{1,0:T(8,128)(2,1)} %get-tuple-element.24.refs_1_, bf16[512,512]{1,0:T(8,128)(2,1)} %copy-done.2, bf16[512,512]{1,0:T(8,128)(2,1)} %copy-done.1, ...), custom_call_target="tpu_custom_call" | custom-call | flops 524288 | bytes 524288 | tf_op jit(solution)/shard_map/partner_first/pallas_call | solution.py:224
  118.2 1.3 collective-permute-start.22
  119.6 0.8 copy-done.14
  120.3 0.8 copy-done.15
  121.1 1.7 partner_last.1
  122.9 0.7 collective-permute-start.21
  123.6 1.9 own_columns.1
  125.5 61.0 %collective-permute-done.22 = bf16[1024,512]{1,0:T(8,128)(2,1)S(1)} collective-permute-done((bf16[1024,512]{1,0:T(8,128)(2,1)}, bf16[1024,512]{1,0:T(8,128)(2,1)S(1)}, u32[]{:S(2)}, u32[]{:S(2)}) %collective-permute-start.22) | collective-permute-done | bytes 1048608 | tf_op jit(solution)/shard_map/ppermute | solution.py:34
  186.5 1.1 select_select_fusion
  (69 shorter events, 9.0 us)
Async XLA Ops:
  6.5 107.7 %all-gather.2.cloned.1.call-start = ((), (), s32[]{:S(2)}) async-start(), calls=%async_computation | async-start | bytes 8650752 | tf_op jit(solution)/shard_map/all_gather | solution.py:264
  12.3 39.5 %collective-permute-start = (bf16[160,512]{1,0:T(8,128)(2,1)}, bf16[160,512]{1,0:T(8,128)(2,1)S(1)}, u32[]{:S(2)}, u32[]{:S(2)}) collective-permute-start(bf16[160,512]{1,0:T(8,128)(2,1)} %get-tuple-element.26), channel_id=1, source_target_pairs={{0,8},{8,16},{16,24},{24,32},{32,40},{40,48},{48,56},{56,64},{64,7... | collective-permute-start | bytes 491528 | tf_op jit(solution)/shard_map/ppermute | solution.py:259
  51.8 12.5 %collective-permute-start.2 = (bf16[512,512]{1,0:T(8,128)(2,1)}, bf16[512,512]{1,0:T(8,128)(2,1)S(1)}, u32[]{:S(2)}, u32[]{:S(2)}) collective-permute-start(bf16[512,512]{1,0:T(8,128)(2,1)} %get-tuple-element.24.refs_1_), channel_id=1, source_target_pairs={{1,0},{2,1},{3,2},{4,3},{5,4},{6,5},{7,6},{14,15},{13,14},{12,13},... | collective-permute-start | bytes 1572872 | tf_op jit(solution)/shard_map/ppermute | solution.py:26
  60.6 10.2 %collective-permute-start.1 = (bf16[512,512]{1,0:T(8,128)(2,1)}, bf16[512,512]{1,0:T(8,128)(2,1)S(1)}, u32[]{:S(2)}, u32[]{:S(2)}) collective-permute-start(bf16[512,512]{1,0:T(8,128)(2,1)} %early_tokens.1.refs_0_), channel_id=1, source_target_pairs={{1,0},{2,1},{3,2},{4,3},{5,4},{6,5},{7,6},{14,15},{13,14},{12,13},... | collective-permute-start | bytes 1572872 | tf_op jit(solution)/shard_map/ppermute | solution.py:26
  64.4 7.1 %collective-permute-start.4 = (bf16[512,512]{1,0:T(8,128)(2,1)S(1)}, bf16[512,512]{1,0:T(8,128)(2,1)S(1)}, u32[]{:S(2)}, u32[]{:S(2)}) collective-permute-start(bf16[512,512]{1,0:T(8,128)(2,1)S(1)} %collective-permute-done.2.refs_3_), channel_id=1, source_target_pairs={{1,0},{2,1},{3,2},{4,3},{5,4},{6,5},{14,15},{13,14},{12,13},{11,12... | collective-permute-start | bytes 1572872 | tf_op jit(solution)/shard_map/ppermute | solution.py:26
  70.7 1.4 collective-permute-start.3
  71.4 2.8 %collective-permute-start.6 = (bf16[512,512]{1,0:T(8,128)(2,1)S(1)}, bf16[512,512]{1,0:T(8,128)(2,1)S(1)}, u32[]{:S(2)}, u32[]{:S(2)}) collective-permute-start(bf16[512,512]{1,0:T(8,128)(2,1)S(1)} %collective-permute-done.4.refs_5_), channel_id=1, source_target_pairs={{1,0},{2,1},{3,2},{4,3},{5,4},{14,15},{13,14},{12,13},{11,12},{10,... | collective-permute-start | bytes 1572872 | tf_op jit(solution)/shard_map/ppermute | solution.py:26
  72.2 2.8 %collective-permute-start.5 = (bf16[512,512]{1,0:T(8,128)(2,1)S(1)}, bf16[512,512]{1,0:T(8,128)(2,1)S(1)}, u32[]{:S(2)}, u32[]{:S(2)}) collective-permute-start(bf16[512,512]{1,0:T(8,128)(2,1)S(1)} %collective-permute-done.3.refs_4_), channel_id=1, source_target_pairs={{1,0},{2,1},{3,2},{4,3},{5,4},{14,15},{13,14},{12,13},{11,12},{10,... | collective-permute-start | bytes 1572872 | tf_op jit(solution)/shard_map/ppermute | solution.py:26
  72.9 2.9 %collective-permute-start.14 = (bf16[512,512]{1,0:T(8,128)(2,1)S(1)}, bf16[512,512]{1,0:T(8,128)(2,1)S(1)}, u32[]{:S(2)}, u32[]{:S(2)}) collective-permute-start(bf16[512,512]{1,0:T(8,128)(2,1)S(1)} %copy-done), channel_id=1, source_target_pairs={{0,1},{1,2},{2,3},{15,14},{14,13},{13,12},{16,17},{17,18},{18,19},... | collective-permute-start | bytes 1572872 | tf_op jit(solution)/shard_map/ppermute | solution.py:30
  73.6 2.9 %collective-permute-start.11 = (bf16[512,512]{1,0:T(8,128)(2,1)}, bf16[512,512]{1,0:T(8,128)(2,1)S(1)}, u32[]{:S(2)}, u32[]{:S(2)}) collective-permute-start(bf16[512,512]{1,0:T(8,128)(2,1)} %early_tokens.1.refs_0_), channel_id=1, source_target_pairs={{0,1},{1,2},{2,3},{15,14},{14,13},{13,12},{16,17},{17,18},{18,19},... | collective-permute-start | bytes 1572872 | tf_op jit(solution)/shard_map/ppermute | solution.py:30
  74.3 2.9 %collective-permute-start.8 = (bf16[512,512]{1,0:T(8,128)(2,1)S(1)}, bf16[512,512]{1,0:T(8,128)(2,1)S(1)}, u32[]{:S(2)}, u32[]{:S(2)}) collective-permute-start(bf16[512,512]{1,0:T(8,128)(2,1)S(1)} %collective-permute-done.6.refs_7_), channel_id=1, source_target_pairs={{1,0},{2,1},{3,2},{4,3},{14,15},{13,14},{12,13},{11,12},{17,16},{1... | collective-permute-start | bytes 1572872 | tf_op jit(solution)/shard_map/ppermute | solution.py:26
  75.0 3.7 %collective-permute-start.7 = (bf16[512,512]{1,0:T(8,128)(2,1)S(1)}, bf16[512,512]{1,0:T(8,128)(2,1)S(1)}, u32[]{:S(2)}, u32[]{:S(2)}) collective-permute-start(bf16[512,512]{1,0:T(8,128)(2,1)S(1)} %collective-permute-done.5.refs_6_), channel_id=1, source_target_pairs={{1,0},{2,1},{3,2},{4,3},{14,15},{13,14},{12,13},{11,12},{17,16},{1... | collective-permute-start | bytes 1572872 | tf_op jit(solution)/shard_map/ppermute | solution.py:26
  75.7 4.4 %collective-permute-start.15 = (bf16[512,512]{1,0:T(8,128)(2,1)S(1)}, bf16[512,512]{1,0:T(8,128)(2,1)S(1)}, u32[]{:S(2)}, u32[]{:S(2)}) collective-permute-start(bf16[512,512]{1,0:T(8,128)(2,1)S(1)} %collective-permute-done.14.refs_17_.refs_21_), channel_id=1, source_target_pairs={{1,2},{2,3},{14,13},{13,12},{17,18},{18,19},{30,29},{29,28},{33,34... | collective-permute-start | bytes 1572872 | tf_op jit(solution)/shard_map/ppermute | solution.py:30
  76.5 4.4 %collective-permute-start.12 = (bf16[512,512]{1,0:T(8,128)(2,1)S(1)}, bf16[512,512]{1,0:T(8,128)(2,1)S(1)}, u32[]{:S(2)}, u32[]{:S(2)}) collective-permute-start(bf16[512,512]{1,0:T(8,128)(2,1)S(1)} %collective-permute-done.11.refs_16_.refs_20_), channel_id=1, source_target_pairs={{1,2},{2,3},{14,13},{13,12},{17,18},{18,19},{30,29},{29,28},{33,34... | collective-permute-start | bytes 1572872 | tf_op jit(solution)/shard_map/ppermute | solution.py:30
  77.2 5.1 %collective-permute-start.10 = (bf16[512,512]{1,0:T(8,128)(2,1)S(1)}, bf16[512,512]{1,0:T(8,128)(2,1)}, u32[]{:S(2)}, u32[]{:S(2)}) collective-permute-start(bf16[512,512]{1,0:T(8,128)(2,1)S(1)} %collective-permute-done.8.refs_9_), channel_id=1, source_target_pairs={{1,0},{2,1},{3,2},{14,15},{13,14},{12,13},{17,16},{18,17},{19,18},... | collective-permute-start | bytes 1572872 | tf_op jit(solution)/shard_map/ppermute | solution.py:26
  78.7 5.1 %collective-permute-start.9 = (bf16[512,512]{1,0:T(8,128)(2,1)S(1)}, bf16[512,512]{1,0:T(8,128)(2,1)}, u32[]{:S(2)}, u32[]{:S(2)}) collective-permute-start(bf16[512,512]{1,0:T(8,128)(2,1)S(1)} %collective-permute-done.7.refs_8_), channel_id=1, source_target_pairs={{1,0},{2,1},{3,2},{14,15},{13,14},{12,13},{17,16},{18,17},{19,18},... | collective-permute-start | bytes 1572872 | tf_op jit(solution)/shard_map/ppermute | solution.py:26
  80.1 5.1 %collective-permute-start.16 = (bf16[512,512]{1,0:T(8,128)(2,1)S(1)}, bf16[512,512]{1,0:T(8,128)(2,1)S(1)}, u32[]{:S(2)}, u32[]{:S(2)}) collective-permute-start(bf16[512,512]{1,0:T(8,128)(2,1)S(1)} %collective-permute-done.15.refs_15_.refs_17_), channel_id=1, source_target_pairs={{2,3},{13,12},{18,19},{29,28},{34,35},{45,44},{50,51},{61,60},{66,... | collective-permute-start | bytes 1572872 | tf_op jit(solution)/shard_map/ppermute | solution.py:30
  80.9 5.2 %collective-permute-start.13 = (bf16[512,512]{1,0:T(8,128)(2,1)S(1)}, bf16[512,512]{1,0:T(8,128)(2,1)}, u32[]{:S(2)}, u32[]{:S(2)}) collective-permute-start(bf16[512,512]{1,0:T(8,128)(2,1)S(1)} %collective-permute-done.12.refs_14_.refs_16_), channel_id=1, source_target_pairs={{2,3},{13,12},{18,19},{29,28},{34,35},{45,44},{50,51},{61,60},{66,... | collective-permute-start | bytes 1572872 | tf_op jit(solution)/shard_map/ppermute | solution.py:30
  82.3 34.5 %collective-permute-start.18 = (bf16[512,512]{1,0:T(8,128)(2,1)}, bf16[512,512]{1,0:T(8,128)(2,1)}, u32[]{:S(2)}, u32[]{:S(2)}) collective-permute-start(bf16[512,512]{1,0:T(8,128)(2,1)} %collective-permute-done.10.refs_11_), channel_id=1, source_target_pairs={{1,0},{2,1},{14,15},{13,14},{17,16},{18,17},{30,31},{29,30},{33,32... | collective-permute-start | bytes 1572872 | tf_op jit(solution)/shard_map/ppermute | solution.py:26
  83.8 33.0 %collective-permute-start.17 = (bf16[512,512]{1,0:T(8,128)(2,1)}, bf16[512,512]{1,0:T(8,128)(2,1)}, u32[]{:S(2)}, u32[]{:S(2)}) collective-permute-start(bf16[512,512]{1,0:T(8,128)(2,1)} %collective-permute-done.9.refs_10_), channel_id=1, source_target_pairs={{1,0},{2,1},{14,15},{13,14},{17,16},{18,17},{30,31},{29,30},{33,32... | collective-permute-start | bytes 1572872 | tf_op jit(solution)/shard_map/ppermute | solution.py:26
  116.8 2.7 %collective-permute-start.19 = (bf16[512,512]{1,0:T(8,128)(2,1)}, bf16[512,512]{1,0:T(8,128)(2,1)S(1)}, u32[]{:S(2)}, u32[]{:S(2)}) collective-permute-start(bf16[512,512]{1,0:T(8,128)(2,1)} %collective-permute-done.17.refs_14_.refs_0_), channel_id=1, source_target_pairs={{1,0},{14,15},{17,16},{30,31},{33,32},{46,47},{49,48},{62,63},{65,... | collective-permute-start | bytes 1572872 | tf_op jit(solution)/shard_map/ppermute | solution.py:26
  117.5 2.0 %collective-permute-start.20 = (bf16[512,512]{1,0:T(8,128)(2,1)}, bf16[512,512]{1,0:T(8,128)(2,1)S(1)}, u32[]{:S(2)}, u32[]{:S(2)}) collective-permute-start(bf16[512,512]{1,0:T(8,128)(2,1)} %collective-permute-done.18.refs_15_.refs_1_), channel_id=1, source_target_pairs={{1,0},{14,15},{17,16},{30,31},{33,32},{46,47},{49,48},{62,63},{65,... | collective-permute-start | bytes 1572872 | tf_op jit(solution)/shard_map/ppermute | solution.py:26
  118.2 68.3 %collective-permute-start.22 = (bf16[1024,512]{1,0:T(8,128)(2,1)}, bf16[1024,512]{1,0:T(8,128)(2,1)S(1)}, u32[]{:S(2)}, u32[]{:S(2)}) collective-permute-start(bf16[1024,512]{1,0:T(8,128)(2,1)} %get-tuple-element.40), channel_id=1, source_target_pairs={{2,6},{3,7},{13,9},{12,8},{18,22},{19,23},{29,25},{28,24},{34,38},... | collective-permute-start | bytes 3145736 | tf_op jit(solution)/shard_map/ppermute | solution.py:34
  122.9 63.6 %collective-permute-start.21 = (bf16[1024,512]{1,0:T(8,128)(2,1)}, bf16[1024,512]{1,0:T(8,128)(2,1)S(1)}, u32[]{:S(2)}, u32[]{:S(2)}) collective-permute-start(bf16[1024,512]{1,0:T(8,128)(2,1)} %partner_last.1), channel_id=1, source_target_pairs={{0,4},{1,5},{15,11},{14,10},{16,20},{17,21},{31,27},{30,26},{32,36... | collective-permute-start | bytes 3145736 | tf_op jit(solution)/shard_map/ppermute | solution.py:34
  (18 other events, 361.2 us)
Sparse Core Ops, SparseCore 0:
  51.9 62.2 all-gather.1
